TPU v7x, 32 devices: a whole 2x2x4 slice. The times are simulated.
32 devices in a mesh: band: 16 (over z, x, core), var: 2 (over y).
Axes of the slice: x: 2, y: 2, z: 4, core: 2. Of those that a mesh axis runs over, the one named last changes fastest.
Arguments:
- patches: bfloat16 [16, 16, 64, 64], P('var', 'band'), may hold values from -6 to 6
- w_embed: bfloat16 [16, 64, 2048], P('var'), may hold values from -0.75 to 0.75
- var_bias: float32 [16, 2048], P('var'), may hold values from -3 to 3
- agg_gain: float32 [2048], replicated, may hold values from 0.1 to 1.9
- wq: bfloat16 [2048, 2048], P(None, 'var'), may hold values from -4 to 4
- wk: bfloat16 [2048, 2048], P(None, 'var'), may hold values from -4 to 4
- wv: bfloat16 [2048, 2048], P(None, 'var'), may hold values from -0.125 to 0.125
- wo: bfloat16 [2048, 2048], P('var'), may hold values from -0.125 to 0.125
- w_up: bfloat16 [2048, 1024], replicated, may hold values from -0.125 to 0.125
- conv1: bfloat16 [9, 64, 64], replicated, may hold values from -0.25 to 0.25
- bias1: float32 [64], replicated, may hold values from -3 to 3
- conv2: bfloat16 [9, 64, 64], replicated, may hold values from -0.25 to 0.25
- cotangent: bfloat16 [64, 64, 256], P('band', None, 'var'), may hold values from -6 to 6
Outputs:
- field_out: bfloat16 [64, 64, 256], P('band', None, 'var')
- grad_fine: bfloat16 [64, 64, 256], P('band', None, 'var')
- grad_conv1: float32 [9, 64, 64], replicated
- grad_conv2: float32 [9, 64, 64], replicated
- grad_bias: float32 [64], replicated
All inputs are finite; a program needn't handle non-finite values.
Results may differ from a plain program's by a relative error of at most 0.03.
Values may be sent and summed in bfloat16 or wider, within the bound.
A program may use at most 128 MiB of HBM per device.

v0:
```python
import math

import jax
import jax.numpy as jnp
from jax import lax
from jax.sharding import PartitionSpec as P

D = 2048
HD = 128
C = 64
R = 4


def with_halo(cells, sides, width):
    for axis, dim in sides:
        count = lax.axis_size(axis)
        ends = count - 1
        head = lax.slice_in_dim(cells, 0, width, axis=dim)
        tail = lax.slice_in_dim(cells, cells.shape[dim] - width, cells.shape[dim], axis=dim)
        cells = jnp.concatenate(
            [
                lax.ppermute(tail, axis, [(i, (i + 1) % count) for i in range(ends)]),
                cells,
                lax.ppermute(head, axis, [((i + 1) % count, i) for i in range(ends)]),
            ],
            axis=dim,
        )
    return cells


def tap_stack(padded, height, width):
    pieces = [
        padded[row_tap : row_tap + height, :, col_tap : col_tap + width]
        for row_tap in range(3)
        for col_tap in range(3)
    ]
    return jnp.concatenate(pieces, axis=1)


def conv_padded(padded, weight, height, width):
    stacked = tap_stack(padded, height, width)
    return jnp.einsum(
        "ykx,ko->yox",
        stacked,
        weight.reshape(-1, weight.shape[2]),
        preferred_element_type=jnp.float32,
    )


def flipped(weight):
    return jnp.transpose(weight[::-1], (0, 2, 1))


def weight_grad(padded, grads):
    stacked = tap_stack(padded, grads.shape[0], grads.shape[2])
    summed = jnp.einsum("ykx,yox->ko", stacked, grads, preferred_element_type=jnp.float32)
    return summed.reshape(9, padded.shape[1], grads.shape[1])


def normalize(mixed, agg_gain):
    return (
        mixed * lax.rsqrt(jnp.mean(mixed * mixed, axis=-1, keepdims=True) + 1e-05) * agg_gain
    ).astype(jnp.bfloat16)


def gradient_rim(field):
    return with_halo(field, (("band", 0), ("var", 2)), 1)


def on_device(
    patches, w_embed, var_bias, agg_gain, wq, wk, wv, wo, w_up, conv1, bias1, conv2, cotangent
):
    var_count = lax.axis_size("var")
    band_count = lax.axis_size("band")
    var_local, lat_dev, lon_all, patch_len = patches.shape
    lon_dev = lon_all // var_count
    flattened = jnp.transpose(patches, (1, 2, 0, 3)).reshape(
        lat_dev * lon_all, var_local * patch_len
    )
    partial_mix = jnp.dot(
        flattened, w_embed.reshape(var_local * patch_len, D), preferred_element_type=jnp.float32
    )
    partial_mix = (partial_mix + jnp.sum(var_bias, axis=0)).reshape(lat_dev, lon_all, D)
    mixed = lax.psum(partial_mix.astype(jnp.bfloat16), "var").astype(jnp.float32)
    normed_band = normalize(mixed, agg_gain)
    normed_slab = lax.dynamic_slice_in_dim(normed_band, lax.axis_index("var") * lon_dev, lon_dev, 1)
    token_rows = jnp.transpose(
        normed_band.reshape(lat_dev, var_count, lon_dev, D), (1, 0, 2, 3)
    ).reshape(-1, D)
    heads_local = wq.shape[1] // HD
    query_rows = token_rows.shape[0]
    queries = jnp.dot(token_rows, wq, preferred_element_type=jnp.float32).astype(jnp.bfloat16)
    keys_local = jnp.dot(token_rows, wk, preferred_element_type=jnp.float32).astype(jnp.bfloat16)
    values_local = jnp.dot(token_rows, wv, preferred_element_type=jnp.float32).astype(jnp.bfloat16)
    query_heads = queries.reshape(query_rows, heads_local, HD)
    running_max = jnp.full((heads_local, query_rows), -1e30, jnp.float32)
    key_heads = lax.all_gather(keys_local, "band", axis=0, tiled=True).reshape(-1, heads_local, HD)
    value_heads = lax.all_gather(values_local, "band", axis=0, tiled=True).reshape(
        -1, heads_local, HD
    )
    scores = jnp.einsum(
        "qhd,khd->hqk", query_heads, key_heads, preferred_element_type=jnp.float32
    ) / math.sqrt(HD)
    new_max = jnp.maximum(running_max, jnp.max(scores, axis=2))
    weights = jnp.exp(scores - new_max[:, :, None])
    new_sum = jnp.sum(weights, axis=2)
    update = jnp.einsum(
        "hqk,khd->hqd",
        weights.astype(jnp.bfloat16),
        value_heads,
        preferred_element_type=jnp.float32,
    )
    context = (update / new_sum[:, :, None]).astype(jnp.bfloat16)
    context = jnp.transpose(context, (1, 0, 2)).reshape(query_rows, heads_local * HD)
    slab_rows = lat_dev * lon_dev
    attended = lax.psum_scatter(
        jnp.dot(context, wo, preferred_element_type=jnp.float32).astype(jnp.bfloat16),
        "var",
        scatter_dimension=0,
        tiled=True,
    ).astype(jnp.float32)
    hidden = (normed_slab.reshape(slab_rows, D).astype(jnp.float32) + attended).astype(jnp.bfloat16)
    upsampled = jnp.dot(hidden, w_up, preferred_element_type=jnp.float32).astype(jnp.bfloat16)
    height = lat_dev * R
    width = lon_dev * R
    upsampled = jnp.transpose(
        upsampled.reshape(lat_dev, lon_dev, R, R, C), (0, 2, 4, 1, 3)
    ).reshape(height, C, width)
    bias_cols = bias1[None, :, None]
    widened = with_halo(upsampled, (("band", 0), ("var", 2)), 2)
    pre_wide = conv_padded(widened, conv1, height + 2, width + 2) + bias_cols
    row_ids = lax.axis_index("band") * height + jnp.arange(height + 2) - 1
    col_ids = lax.axis_index("var") * width + jnp.arange(width + 2) - 1
    rows_inside = (row_ids >= 0) & (row_ids < height * band_count)
    cols_inside = (col_ids >= 0) & (col_ids < width * var_count)
    inside = rows_inside[:, None, None] & cols_inside[None, None, :]
    active_pad = jnp.where(inside, jax.nn.gelu(pre_wide), 0.0).astype(jnp.bfloat16)
    fine_pad = widened[1:-1, :, 1:-1]
    pre = pre_wide[1:-1, :, 1:-1]
    field_out = (
        conv_padded(active_pad, conv2, height, width) + upsampled.astype(jnp.float32)
    ).astype(jnp.bfloat16)
    cotangent_pad = gradient_rim(cotangent)
    d_active = conv_padded(cotangent_pad, flipped(conv2), height, width)
    d_pre = jax.vjp(jax.nn.gelu, pre)[1](d_active)[0].astype(jnp.bfloat16)
    d_pre_pad = gradient_rim(d_pre)
    grad_fine = (
        cotangent.astype(jnp.float32) + conv_padded(d_pre_pad, flipped(conv1), height, width)
    ).astype(jnp.bfloat16)
    factor = 1.0 / math.sqrt(height * band_count * width * var_count)
    first_terms = weight_grad(fine_pad, d_pre) * factor
    second_terms = weight_grad(active_pad, cotangent) * factor
    bias_terms = jnp.sum(d_pre.astype(jnp.float32), axis=(0, 2)) * factor
    grad_conv1, grad_conv2, grad_bias = lax.psum(
        (first_terms, second_terms, bias_terms), ("band", "var")
    )
    return (field_out, grad_fine, grad_conv1, grad_conv2, grad_bias)


def solution(mesh):
    in_specs = (
        P("var", "band", None, None),
        P("var", None, None),
        P("var", None),
        P(),
        P(None, "var"),
        P(None, "var"),
        P(None, "var"),
        P("var", None),
        P(),
        P(),
        P(),
        P(),
        P("band", None, "var"),
    )
    out_specs = (P("band", None, "var"), P("band", None, "var"), P(), P(), P())
    return jax.shard_map(
        on_device, mesh=mesh, in_specs=in_specs, out_specs=out_specs, check_vma=False
    )
```

profile of v0, /device:TPU:25, one launch (start us, length us, event | category | flops | bytes accessed | tf_op | source)
XLA Modules:
  0.0 326.4 jit_solution(15782419090284426624)
XLA Ops:
  10.7 24.0 %all-reduce.4.cloned.1.call-done = bf16[1,64,2048]{2,1,0:T(8,128)(2,1)} async-done(((bf16[1,64,2048]{2,1,0:T(8,128)(2,1)}), bf16[1,64,2048]{2,1,0:T(8,128)(2,1)}) %all-reduce.4.cloned.1.call-update) | async-done | bytes 262160 | tf_op jit(solution)/shard_map/psum | solution.py:84
  36.8 3.7 %convolution_convert_fusion.2 = bf16[64,1024]{1,0:T(8,128)(2,1)} fusion(bf16[2048,1024]{1,0:T(8,128)(2,1)} %param.18, bf16[1,64,2048]{2,1,0:T(8,128)(2,1)S(1)} %fusion.35), kind=kOutput, calls=%fused_computation.22 | convolution fusion | flops 268500992 | bytes 4587520 | tf_op jit(solution)/shard_map/dot_general | solution.py:93
  40.7 3.8 %convolution_convert_fusion.1 = bf16[64,1024]{1,0:T(8,128)(2,1)} fusion(bf16[2048,1024]{1,0:T(8,128)(2,1)} %param.19, bf16[1,64,2048]{2,1,0:T(8,128)(2,1)S(1)} %fusion.35), kind=kOutput, calls=%fused_computation.21 | convolution fusion | flops 268500992 | bytes 4587520 | tf_op jit(solution)/shard_map/dot_general | solution.py:94
  44.5 4.1 %collective-permute-start.4 = (bf16[1,64,128]{2,1,0:T(8,128)(2,1)S(1)}, bf16[1,64,128]{2,1,0:T(8,128)(2,1)S(1)}, u32[]{:S(2)}, u32[]{:S(2)}) collective-permute-start(bf16[1,64,128]{2,1,0:T(8,128)(2,1)S(1)} %get-tuple-element.49), channel_id=1, source_target_pairs={{0,2},{2,4},{4,6},{6,8},{8,10},{10,12},{12,14},{14,16},{16,18},{18... | collective-permute-start | bytes 49160 | tf_op jit(solution)/shard_map/ppermute | solution.py:22
  48.6 1.9 collective-permute-start.5
  50.7 3.0 collective-permute-done.5
  53.8 2.6 collective-permute-start.6
  60.7 3.8 %collective-permute-done.7 = bf16[6,64,1]{2,1,0:T(8,128)(2,1)S(1)} collective-permute-done((bf16[6,64,1]{2,1,0:T(8,128)(2,1)S(1)}, bf16[6,64,1]{2,1,0:T(8,128)(2,1)S(1)}, u32[]{:S(2)}, u32[]{:S(2)}) %collective-permute-start.7) | collective-permute-done | bytes 800 | tf_op jit(solution)/shard_map/ppermute | solution.py:24
  65.3 3.3 %fusion.24 = bf16[8,8,8,128]{3,2,1,0:T(8,128)(2,1)S(1)} fusion(bf16[2048,1024]{1,0:T(8,128)(2,1)} %param.17, bf16[1,64,2048]{2,1,0:T(8,128)(2,1)S(1)} %fusion.35), kind=kOutput, calls=%fused_computation.29 | convolution fusion | flops 268500992 | bytes 4587520 | tf_op jit(solution)/shard_map/dot_general | solution.py:92
  68.5 13.2 %all-gather.3.cloned.1.call-done = bf16[1024,1024]{1,0:T(8,128)(2,1)} async-done(((bf16[64,1024]{1,0:T(8,128)(2,1)}), bf16[1024,1024]{1,0:T(8,128)(2,1)}) %all-gather.3.cloned.1.call-update) | async-done | bytes 2097168 | tf_op jit(solution)/shard_map/all_gather | solution.py:97
  81.8 2.5 multiply_reduce_fusion
  86.1 38.9 %all-gather.5.cloned.1.call-done = bf16[1024,1024]{1,0:T(8,128)(2,1)} async-done(((bf16[64,1024]{1,0:T(8,128)(2,1)}), bf16[1024,1024]{1,0:T(8,128)(2,1)}) %all-gather.5.cloned.1.call-update) | async-done | bytes 2097168 | tf_op jit(solution)/shard_map/all_gather | solution.py:98
  125.0 3.2 fusion.26
  128.4 1.5 convolution_convert_fusion
  133.5 7.9 %reduce-scatter.2.cloned.1.call-done = bf16[32,2048]{1,0:T(8,128)(2,1)} async-done(((bf16[64,2048]{1,0:T(8,128)(2,1)}), bf16[32,2048]{1,0:T(8,128)(2,1)}) %reduce-scatter.2.cloned.1.call-update) | async-done | bytes 131088 | tf_op jit(solution)/shard_map/reduce_scatter | solution.py:116
  141.4 3.1 convolution_convert_fusion.4
  144.8 3.7 %collective-permute-start = (bf16[2,64,128]{1,2,0:T(8,128)(2,1)S(1)}, bf16[2,64,128]{1,2,0:T(8,128)(2,1)S(1)}, u32[]{:S(2)}, u32[]{:S(2)}) collective-permute-start(bf16[2,64,128]{1,2,0:T(8,128)(2,1)S(1)} %bitcast.147), channel_id=1, source_target_pairs={{0,2},{2,4},{4,6},{6,8},{8,10},{10,12},{12,14},{14,16},{16,18},{18... | collective-permute-start | bytes 98312 | tf_op jit(solution)/shard_map/ppermute | solution.py:22
  148.5 1.9 collective-permute-start.1
  151.2 2.9 collective-permute-done.1
  154.1 2.2 collective-permute-start.2
  158.3 2.3 collective-permute-done.3
  163.5 3.3 %concatenate.88 = bf16[6,576,130]{1,2,0:T(8,128)(2,1)} concatenate(bf16[6,64,130]{1,2,0:T(8,128)(2,1)S(1)} %get-tuple-element.59, bf16[6,64,130]{1,2,0:T(8,128)(2,1)} %get-tuple-element.28, bf16[6,64,130]{1,2,0:T(8,128)(2,1)S(1)} %get-tuple-element.25, bf16[6,64,130]{1,2,0:T(8,128)(2,1)S(1)} %get-tuple-element.60, bf16[6,64,130]{1,2,0:T(8,128)(2,1)} %get-tuple-element.27, ...), dimensions={1} | concatenate | bytes 1797120 | tf_op jit(solution)/shard_map/concatenate | solution.py:37
  166.8 1.9 fusion.44
  168.7 2.0 convert_reduce_fusion
  171.4 1.4 concatenate.104
  173.8 3.3 %collective-permute-start.8 = (bf16[1,64,128]{2,1,0:T(8,128)(2,1)}, bf16[1,64,128]{2,1,0:T(8,128)(2,1)S(1)}, u32[]{:S(2)}, u32[]{:S(2)}) collective-permute-start(bf16[1,64,128]{2,1,0:T(8,128)(2,1)} %get-tuple-element.46), channel_id=1, source_target_pairs={{0,2},{2,4},{4,6},{6,8},{8,10},{10,12},{12,14},{14,16},{16,18},{18... | collective-permute-start | bytes 49160 | tf_op jit(solution)/shard_map/ppermute | solution.py:22
  177.1 1.9 collective-permute-start.9
  179.7 2.4 collective-permute-done.9
  187.4 39.8 %psum.31 = f32[64]{0:T(128)} all-reduce(f32[64]{0:T(128)S(1)} %broadcast_multiply_fusion), channel_id=1, replica_groups=mesh['band'=16,'var'=2] {'band','var'}, use_global_device_ids=true, to_apply=%region_9.10 | all-reduce | flops 64 | bytes 512 | tf_op jit(solution)/shard_map/psum | solution.py:154
  228.8 87.7 %all-reduce.6.cloned.1.call-done = (f32[9,64,64]{2,1,0:T(8,128)}, f32[9,64,64]{2,1,0:T(8,128)}) async-done(((f32[9,64,64]{2,1,0:T(8,128)}, f32[9,64,64]{2,1,0:T(8,128)}), (f32[9,64,64]{2,1,0:T(8,128)}, f32[9,64,64]{2,1,0:T(8,128)})) %all-reduce.6.cloned.1.call-update) | async-done | bytes 294928 | tf_op jit(solution)/shard_map/psum | solution.py:154
  316.4 1.7 copy.121
  318.1 1.7 copy.122
  (117 shorter events, 31.5 us)
Async XLA Ops:
  7.2 2.2 copy-start
  7.2 28.6 %copy-start.9 = (f32[2048]{0:T(1024)S(1)}, f32[2048]{0:T(1024)}, u32[]{:S(2)}) copy-start(f32[2048]{0:T(1024)} %param.16) | copy-start | bytes 24580
  7.2 27.4 %all-reduce.4.cloned.1.call-start = ((), (), s32[]{:S(2)}) async-start(), calls=%async_computation.1 | async-start | bytes 524288 | tf_op jit(solution)/shard_map/psum | solution.py:84
  10.6 71.2 %all-gather.3.cloned.1.call-start = ((), (), s32[]{:S(2)}) async-start(), calls=%async_computation.2 | async-start | bytes 2228224 | tf_op jit(solution)/shard_map/all_gather | solution.py:97
  40.6 3.9 %copy-start.3 = (bf16[4,64,128]{2,1,0:T(8,128)(2,1)S(1)}, bf16[4,64,128]{2,1,0:T(8,128)(2,1)}, u32[]{:S(2)}) copy-start(bf16[4,64,128]{2,1,0:T(8,128)(2,1)} %param.25) | copy-start | bytes 196612
  40.6 10.1 %copy-start.4 = (bf16[9,64,64]{2,1,0:T(8,128)(2,1)S(1)}, bf16[9,64,64]{2,1,0:T(8,128)(2,1)}, u32[]{:S(2)}) copy-start(bf16[9,64,64]{2,1,0:T(8,128)(2,1)} %param.24) | copy-start | bytes 221188
  40.6 15.8 %copy-start.7 = (bf16[9,64,64]{2,1,0:T(8,128)(2,1)S(1)}, bf16[9,64,64]{2,1,0:T(8,128)(2,1)}, u32[]{:S(2)}) copy-start(bf16[9,64,64]{2,1,0:T(8,128)(2,1)} %param.22) | copy-start | bytes 221188
  40.6 84.4 %all-gather.5.cloned.1.call-start = ((), (), s32[]{:S(2)}) async-start(), calls=%async_computation.3 | async-start | bytes 2228224 | tf_op jit(solution)/shard_map/all_gather | solution.py:98
  44.5 97.0 %reduce-scatter.2.cloned.1.call-start = ((), (), s32[]{:S(2)}) async-start(), calls=%async_computation.4 | async-start | bytes 393216 | tf_op jit(solution)/shard_map/reduce_scatter | solution.py:116
  44.5 6.2 %collective-permute-start.4 = (bf16[1,64,128]{2,1,0:T(8,128)(2,1)S(1)}, bf16[1,64,128]{2,1,0:T(8,128)(2,1)S(1)}, u32[]{:S(2)}, u32[]{:S(2)}) collective-permute-start(bf16[1,64,128]{2,1,0:T(8,128)(2,1)S(1)} %get-tuple-element.49), channel_id=1, source_target_pairs={{0,2},{2,4},{4,6},{6,8},{8,10},{10,12},{12,14},{14,16},{16,18},{18... | collective-permute-start | bytes 49160 | tf_op jit(solution)/shard_map/ppermute | solution.py:22
  48.6 5.1 %collective-permute-start.5 = (bf16[1,64,128]{2,1,0:T(8,128)(2,1)S(1)}, bf16[1,64,128]{2,1,0:T(8,128)(2,1)S(1)}, u32[]{:S(2)}, u32[]{:S(2)}) collective-permute-start(bf16[1,64,128]{2,1,0:T(8,128)(2,1)S(1)} %get-tuple-element.48), channel_id=1, source_target_pairs={{2,0},{4,2},{6,4},{8,6},{10,8},{12,10},{14,12},{16,14},{18,16},{20... | collective-permute-start | bytes 49160 | tf_op jit(solution)/shard_map/ppermute | solution.py:24
  53.8 5.5 %collective-permute-start.6 = (bf16[6,64,1]{2,1,0:T(8,128)(2,1)S(1)}, bf16[6,64,1]{2,1,0:T(8,128)(2,1)S(1)}, u32[]{:S(2)}, u32[]{:S(2)}) collective-permute-start(bf16[6,64,1]{2,1,0:T(8,128)(2,1)S(1)} %get-tuple-element.45), channel_id=1, source_target_pairs={{0,1},{2,3},{4,5},{6,7},{8,9},{10,11},{12,13},{14,15},{16,17},{18,... | collective-permute-start | bytes 2312 | tf_op jit(solution)/shard_map/ppermute | solution.py:22
  58.0 6.5 %collective-permute-start.7 = (bf16[6,64,1]{2,1,0:T(8,128)(2,1)S(1)}, bf16[6,64,1]{2,1,0:T(8,128)(2,1)S(1)}, u32[]{:S(2)}, u32[]{:S(2)}) collective-permute-start(bf16[6,64,1]{2,1,0:T(8,128)(2,1)S(1)} %get-tuple-element.44), channel_id=1, source_target_pairs={{1,0},{3,2},{5,4},{7,6},{9,8},{11,10},{13,12},{15,14},{17,16},{19,... | collective-permute-start | bytes 2312 | tf_op jit(solution)/shard_map/ppermute | solution.py:24
  84.3 1.3 copy-start.1
  125.0 3.4 %copy-start.2 = (bf16[1024,2048]{1,0:T(8,128)(2,1)S(1)}, bf16[1024,2048]{1,0:T(8,128)(2,1)}, u32[]{:S(2)}) copy-start(bf16[1024,2048]{1,0:T(8,128)(2,1)} %param.20) | copy-start | bytes 12582916
  130.0 186.4 %all-reduce.6.cloned.1.call-start = ((), (), s32[]{:S(2)}) async-start(), calls=%async_computation.5 | async-start | bytes 1179648 | tf_op jit(solution)/shard_map/psum | solution.py:154
  144.8 6.4 %collective-permute-start = (bf16[2,64,128]{1,2,0:T(8,128)(2,1)S(1)}, bf16[2,64,128]{1,2,0:T(8,128)(2,1)S(1)}, u32[]{:S(2)}, u32[]{:S(2)}) collective-permute-start(bf16[2,64,128]{1,2,0:T(8,128)(2,1)S(1)} %bitcast.147), channel_id=1, source_target_pairs={{0,2},{2,4},{4,6},{6,8},{8,10},{10,12},{12,14},{14,16},{16,18},{18... | collective-permute-start | bytes 98312 | tf_op jit(solution)/shard_map/ppermute | solution.py:22
  148.5 5.6 %collective-permute-start.1 = (bf16[2,64,128]{1,2,0:T(8,128)(2,1)S(1)}, bf16[2,64,128]{1,2,0:T(8,128)(2,1)S(1)}, u32[]{:S(2)}, u32[]{:S(2)}) collective-permute-start(bf16[2,64,128]{1,2,0:T(8,128)(2,1)S(1)} %bitcast.148), channel_id=1, source_target_pairs={{2,0},{4,2},{6,4},{8,6},{10,8},{12,10},{14,12},{16,14},{18,16},{20... | collective-permute-start | bytes 98312 | tf_op jit(solution)/shard_map/ppermute | solution.py:24
  154.1 4.2 %collective-permute-start.2 = (bf16[8,64,2]{1,2,0:T(2,128)(2,1)S(1)}, bf16[8,64,2]{1,2,0:T(2,128)(2,1)S(1)}, u32[]{:S(2)}, u32[]{:S(2)}) collective-permute-start(bf16[8,64,2]{1,2,0:T(2,128)(2,1)S(1)} %get-tuple-element.35), channel_id=1, source_target_pairs={{0,1},{2,3},{4,5},{6,7},{8,9},{10,11},{12,13},{14,15},{16,17},{18,... | collective-permute-start | bytes 6152 | tf_op jit(solution)/shard_map/ppermute | solution.py:22
  156.2 4.4 %collective-permute-start.3 = (bf16[8,64,2]{1,2,0:T(2,128)(2,1)S(1)}, bf16[8,64,2]{1,2,0:T(2,128)(2,1)S(1)}, u32[]{:S(2)}, u32[]{:S(2)}) collective-permute-start(bf16[8,64,2]{1,2,0:T(2,128)(2,1)S(1)} %get-tuple-element.34), channel_id=1, source_target_pairs={{1,0},{3,2},{5,4},{7,6},{9,8},{11,10},{13,12},{15,14},{17,16},{19,... | collective-permute-start | bytes 6152 | tf_op jit(solution)/shard_map/ppermute | solution.py:24
  162.6 4.2 %copy-start.10 = (f32[64]{0:T(128)S(1)}, f32[64]{0:T(128)}, u32[]{:S(2)}) copy-start(f32[64]{0:T(128)} %param.23) | copy-start | bytes 772
  166.8 1.9 copy-start.8
  170.7 8.3 %copy-start.5 = (bf16[9,64,64]{2,1,0:T(8,128)(2,1)S(1)}, bf16[9,64,64]{2,1,0:T(8,128)(2,1)}, u32[]{:S(2)}) copy-start(bf16[9,64,64]{2,1,0:T(8,128)(2,1)} %param.24) | copy-start | bytes 221188
  172.8 12.1 %copy-start.11 = (f32[64]{0:T(128)S(1)}, f32[64]{0:T(128)}, u32[]{:S(2)}) copy-start(f32[64]{0:T(128)} %get-tuple-element.54) | copy-start | bytes 772
  173.8 5.9 %collective-permute-start.8 = (bf16[1,64,128]{2,1,0:T(8,128)(2,1)}, bf16[1,64,128]{2,1,0:T(8,128)(2,1)S(1)}, u32[]{:S(2)}, u32[]{:S(2)}) collective-permute-start(bf16[1,64,128]{2,1,0:T(8,128)(2,1)} %get-tuple-element.46), channel_id=1, source_target_pairs={{0,2},{2,4},{4,6},{6,8},{8,10},{10,12},{12,14},{14,16},{16,18},{18... | collective-permute-start | bytes 49160 | tf_op jit(solution)/shard_map/ppermute | solution.py:22
  177.1 5.1 %collective-permute-start.9 = (bf16[1,64,128]{2,1,0:T(8,128)(2,1)S(1)}, bf16[1,64,128]{2,1,0:T(8,128)(2,1)S(1)}, u32[]{:S(2)}, u32[]{:S(2)}) collective-permute-start(bf16[1,64,128]{2,1,0:T(8,128)(2,1)S(1)} %get-tuple-element.47), channel_id=1, source_target_pairs={{2,0},{4,2},{6,4},{8,6},{10,8},{12,10},{14,12},{16,14},{18,16},{20... | collective-permute-start | bytes 49160 | tf_op jit(solution)/shard_map/ppermute | solution.py:24
  179.7 48.2 %copy-start.6 = (bf16[9,64,64]{2,1,0:T(8,128)(2,1)S(1)}, bf16[9,64,64]{2,1,0:T(8,128)(2,1)}, u32[]{:S(2)}) copy-start(bf16[9,64,64]{2,1,0:T(8,128)(2,1)} %copy.44) | copy-start | bytes 221188
  182.2 45.0 %collective-permute-start.10 = (bf16[6,64,1]{2,1,0:T(8,128)(2,1)S(1)}, bf16[6,64,1]{2,1,0:T(8,128)(2,1)S(1)}, u32[]{:S(2)}, u32[]{:S(2)}) collective-permute-start(bf16[6,64,1]{2,1,0:T(8,128)(2,1)S(1)} %get-tuple-element.43), channel_id=1, source_target_pairs={{0,1},{2,3},{4,5},{6,7},{8,9},{10,11},{12,13},{14,15},{16,17},{18,... | collective-permute-start | bytes 2312 | tf_op jit(solution)/shard_map/ppermute | solution.py:22
  183.6 43.7 %collective-permute-start.11 = (bf16[6,64,1]{2,1,0:T(8,128)(2,1)S(1)}, bf16[6,64,1]{2,1,0:T(8,128)(2,1)S(1)}, u32[]{:S(2)}, u32[]{:S(2)}) collective-permute-start(bf16[6,64,1]{2,1,0:T(8,128)(2,1)S(1)} %get-tuple-element.42), channel_id=1, source_target_pairs={{1,0},{3,2},{5,4},{7,6},{9,8},{11,10},{13,12},{15,14},{17,16},{19,... | collective-permute-start | bytes 2312 | tf_op jit(solution)/shard_map/ppermute | solution.py:24
Sparse Core Ops, SparseCore 0:
  10.9 23.7 all-reduce.3
  40.7 41.0 all-gather.2
  84.7 40.1 all-gather.4
  130.1 11.2 reduce-scatter.1
  187.6 128.8 all-reduce.5
where the time goes:
time: 331 us; the launch traced here: 326 us
  waiting for transfers between devices  186 us (56%)
  blocking collectives  39.8 us (12%)
  matrix products  28 us (8%)
  starting transfers between devices  27 us (8%)
  local copies, waits for them, and re-layouts  20.5 us (6%)
  between operations  14.3 us (4%)
  other arithmetic  10.5 us (3%)
    psum x1, waiting for transfers between devices, on_device(): lax.psum((first_terms, second_terms, bias_terms), ('band', 'var'))  87.7 us
    psum x1, blocking collectives, on_device(): lax.psum((first_terms, second_terms, bias_terms), ('band', 'var'))  39.8 us
    all_gather x1, waiting for transfers between devices, on_device(): lax.all_gather(values_local, 'band', axis=0, tiled=True)  38.9 us
    psum x1, waiting for transfers between devices, on_device(): lax.psum(partial_mix.astype(jnp.bfloat16), 'var').astype(jnp.float32)  24 us
    ppermute x6, starting transfers between devices, with_halo(): lax.ppermute(tail, axis, [(i, (i + 1) % count) for i in range(ends)])  17.2 us
    ppermute x6, waiting for transfers between devices, with_halo(): lax.ppermute(head, axis, [((i + 1) % count, i) for i in range(ends)])  14.4 us
    all_gather x1, waiting for transfers between devices, on_device(): lax.all_gather(keys_local, 'band', axis=0, tiled=True)  13.2 us
    ppermute x6, starting transfers between devices, with_halo(): lax.ppermute(head, axis, [((i + 1) % count, i) for i in range(ends)])  9.63 us
  transfers between devices with their start and end apart: 17, of which 10 were waited for; matrix products, arithmetic and copies ran while one was open for 7% of the time, Pallas kernels for 0%

commit v1 on v0

--- a/solution.py
+++ b/solution.py
@@ -1,9 +1,14 @@
+import functools
 import math
 
 import jax
 import jax.numpy as jnp
 from jax import lax
+from jax.experimental import pallas as pl
+from jax.experimental.pallas import tpu as pltpu
 from jax.sharding import PartitionSpec as P
+
+MESH = pl.DeviceIdType.MESH
 
 D = 2048
 HD = 128
@@ -67,6 +72,86 @@
     return with_halo(field, (("band", 0), ("var", 2)), 1)
 
 
+def sum_kernel(count, var_count, x_ref, o_ref, landed, send1, recv1, send2, recv2):
+    me = lax.axis_index("band") * var_count + lax.axis_index("var")
+
+    def place(device):
+        return (lax.div(device, var_count), lax.rem(device, var_count))
+
+    def scatter(step):
+        peer = lax.rem(me + step, count)
+        return pltpu.make_async_remote_copy(
+            src_ref=x_ref.at[peer],
+            dst_ref=landed.at[step],
+            send_sem=send1.at[step],
+            recv_sem=recv1.at[step],
+            device_id=place(peer),
+            device_id_type=MESH,
+        )
+
+    def spread(step, owner):
+        return pltpu.make_async_remote_copy(
+            src_ref=o_ref.at[owner],
+            dst_ref=o_ref.at[owner],
+            send_sem=send2.at[step],
+            recv_sem=recv2.at[step],
+            device_id=place(lax.rem(me + step, count)),
+            device_id_type=MESH,
+        )
+
+    barrier = pltpu.get_barrier_semaphore()
+
+    @pl.loop(1, count)
+    def _(step):
+        pl.semaphore_signal(
+            barrier, inc=1, device_id=place(lax.rem(me + step, count)), device_id_type=MESH
+        )
+
+    pl.semaphore_wait(barrier, count - 1)
+
+    @pl.loop(1, count)
+    def _(step):
+        scatter(step).start()
+
+    def add(step, total):
+        scatter(step).wait_recv()
+        return total + landed[step]
+
+    o_ref[me] = lax.fori_loop(1, count, add, x_ref[me])
+
+    @pl.loop(1, count)
+    def _(step):
+        spread(step, me).start()
+
+    @pl.loop(1, count)
+    def _(step):
+        spread(step, lax.rem(me - step + count, count)).wait_recv()
+
+    @pl.loop(1, count)
+    def _(step):
+        scatter(step).wait_send()
+        spread(step, me).wait_send()
+
+
+def sum_everywhere(terms, band_count, var_count):
+    count = band_count * var_count
+    rows = -(-terms.shape[0] // (8 * count)) * 8
+    padded = jnp.pad(terms, ((0, rows * count - terms.shape[0]), (0, 0)))
+    slots = (count, rows, terms.shape[1])
+    summed = pl.pallas_call(
+        functools.partial(sum_kernel, count, var_count),
+        out_shape=jax.ShapeDtypeStruct(slots, jnp.float32),
+        in_specs=[pl.BlockSpec(memory_space=pltpu.VMEM)],
+        out_specs=pl.BlockSpec(memory_space=pltpu.VMEM),
+        scratch_shapes=[pltpu.VMEM(slots, jnp.float32)]
+        + [pltpu.SemaphoreType.DMA((count,)) for _ in range(4)],
+        compiler_params=pltpu.CompilerParams(
+            collective_id=0, has_side_effects=True, vmem_limit_bytes=32 << 20
+        ),
+    )(padded.reshape(slots))
+    return summed.reshape(rows * count, terms.shape[1])
+
+
 def on_device(
     patches, w_embed, var_bias, agg_gain, wq, wk, wv, wo, w_up, conv1, bias1, conv2, cotangent
 ):
@@ -81,7 +166,12 @@
         flattened, w_embed.reshape(var_local * patch_len, D), preferred_element_type=jnp.float32
     )
     partial_mix = (partial_mix + jnp.sum(var_bias, axis=0)).reshape(lat_dev, lon_all, D)
-    mixed = lax.psum(partial_mix.astype(jnp.bfloat16), "var").astype(jnp.float32)
+    own_mix = partial_mix.astype(jnp.bfloat16)
+    if var_count == 2:
+        other_mix = lax.ppermute(own_mix, "var", [(0, 1), (1, 0)])
+        mixed = own_mix.astype(jnp.float32) + other_mix.astype(jnp.float32)
+    else:
+        mixed = lax.psum(own_mix, "var").astype(jnp.float32)
     normed_band = normalize(mixed, agg_gain)
     normed_slab = lax.dynamic_slice_in_dim(normed_band, lax.axis_index("var") * lon_dev, lon_dev, 1)
     token_rows = jnp.transpose(
@@ -148,12 +238,15 @@
         cotangent.astype(jnp.float32) + conv_padded(d_pre_pad, flipped(conv1), height, width)
     ).astype(jnp.bfloat16)
     factor = 1.0 / math.sqrt(height * band_count * width * var_count)
-    first_terms = weight_grad(fine_pad, d_pre) * factor
-    second_terms = weight_grad(active_pad, cotangent) * factor
+    first_terms = weight_grad(fine_pad, d_pre).reshape(9 * C, C) * factor
+    second_terms = weight_grad(active_pad, cotangent).reshape(9 * C, C) * factor
     bias_terms = jnp.sum(d_pre.astype(jnp.float32), axis=(0, 2)) * factor
-    grad_conv1, grad_conv2, grad_bias = lax.psum(
-        (first_terms, second_terms, bias_terms), ("band", "var")
-    )
+    terms = jnp.concatenate([first_terms, second_terms], axis=1)
+    bias_row = jnp.pad(bias_terms, (0, C))[None]
+    summed = sum_everywhere(jnp.concatenate([terms, bias_row], axis=0), band_count, var_count)
+    grad_conv1 = summed[: 9 * C, :C].reshape(9, C, C)
+    grad_conv2 = summed[: 9 * C, C:].reshape(9, C, C)
+    grad_bias = summed[9 * C, :C]
     return (field_out, grad_fine, grad_conv1, grad_conv2, grad_bias)
 
 

time: 331 us -> 209 us (0.63)
  waiting for transfers between devices: 186 us -> 81.2 us
  blocking collectives: 39.8 us -> 0 us
  Pallas kernels: 0 us -> 25.6 us
  starting transfers between devices: 27 us -> 31.4 us
    psum x2 -> x0, waiting for transfers between devices: 112 us -> none  [the longest x1 87.7 us: on_device(): lax.psum((first_terms, second_terms, bias_terms), ('band', 'var'))]
    psum x1 -> x0, blocking collectives: 39.8 us -> none  [on_device(): lax.psum((first_terms, second_terms, bias_terms), ('band', 'var'))]
    pallas_call x0 -> x1, Pallas kernels: none -> 25.6 us  [sum_everywhere(): pl.pallas_call(functools.partial(sum_kernel, count, var_count), out_shape...]
    ppermute x0 -> x1, waiting for transfers between devices: none -> 5.93 us  [on_device(): other_mix = lax.ppermute(own_mix, 'var', [(0, 1), (1, 0)])]
    unnamed x44 -> x41, local copies, waits for them, and re-layouts: 7.2 us -> 4.68 us
  transfers between devices with their start and end apart: 17 -> 16, of which waited for: 10 -> 9; matrix products, arithmetic and copies ran while one was open for 7% -> 11% of each run, Pallas kernels for 0% -> 0%
where the time goes in v1:
time: 209 us; the launch traced here: 207 us
  waiting for transfers between devices  81.2 us (39%)
  starting transfers between devices  31.4 us (15%)
  matrix products  27.7 us (13%)
  Pallas kernels  25.6 us (12%)
  local copies, waits for them, and re-layouts  18.1 us (9%)
  between operations  14.3 us (7%)
  other arithmetic  8.72 us (4%)
    all_gather x1, waiting for transfers between devices, on_device(): lax.all_gather(values_local, 'band', axis=0, tiled=True)  38.6 us
    pallas_call x1, Pallas kernels, sum_everywhere(): pl.pallas_call(functools.partial(sum_kernel, count, var_count), out_shape...  25.6 us
    ppermute x6, starting transfers between devices, with_halo(): lax.ppermute(tail, axis, [(i, (i + 1) % count) for i in range(ends)])  20.2 us
    ppermute x6, waiting for transfers between devices, with_halo(): lax.ppermute(head, axis, [((i + 1) % count, i) for i in range(ends)])  15.5 us
    all_gather x1, waiting for transfers between devices, on_device(): lax.all_gather(keys_local, 'band', axis=0, tiled=True)  13.1 us
    ppermute x6, starting transfers between devices, with_halo(): lax.ppermute(head, axis, [((i + 1) % count, i) for i in range(ends)])  9.79 us
    reduce_scatter x1, waiting for transfers between devices, on_device(): lax.psum_scatter(jnp.dot(context, wo, preferred_element_type=jnp.float32)...  7.92 us
    ppermute x1, waiting for transfers between devices, on_device(): other_mix = lax.ppermute(own_mix, 'var', [(0, 1), (1, 0)])  5.93 us
  transfers between devices with their start and end apart: 16, of which 9 were waited for; matrix products, arithmetic and copies ran while one was open for 11% of the time, Pallas kernels for 0%

profile of v1, /device:TPU:25, one launch (start us, length us, event | category | flops | bytes accessed | tf_op | source)
XLA Modules:
  0.0 207.1 jit_solution(12885536083853391476)
XLA Ops:
  9.9 1.3 collective-permute-start
  11.2 5.9 %collective-permute-done = bf16[1,64,2048]{2,1,0:T(8,128)(2,1)S(1)} collective-permute-done((bf16[1,64,2048]{2,1,0:T(8,128)(2,1)S(1)}, bf16[1,64,2048]{2,1,0:T(8,128)(2,1)S(1)}, u32[]{:S(2)}, u32[]{:S(2)}) %collective-permute-start) | collective-permute-done | bytes 262176 | tf_op jit(solution)/shard_map/ppermute | solution.py:171
  17.5 3.7 %convolution_convert_fusion.2 = bf16[64,1024]{1,0:T(8,128)(2,1)} fusion(bf16[2048,1024]{1,0:T(8,128)(2,1)} %param.18, bf16[1,64,2048]{2,1,0:T(8,128)(2,1)S(1)} %multiply_convert_fusion), kind=kOutput, calls=%fused_computation.22 | convolution fusion | flops 268500992 | bytes 4587520 | tf_op jit(solution)/shard_map/dot_general | solution.py:183
  21.3 3.8 %convolution_convert_fusion.1 = bf16[64,1024]{1,0:T(8,128)(2,1)} fusion(bf16[2048,1024]{1,0:T(8,128)(2,1)} %param.19, bf16[1,64,2048]{2,1,0:T(8,128)(2,1)S(1)} %multiply_convert_fusion), kind=kOutput, calls=%fused_computation.21 | convolution fusion | flops 268500992 | bytes 4587520 | tf_op jit(solution)/shard_map/dot_general | solution.py:184
  25.1 4.6 %collective-permute-start.5 = (bf16[1,64,128]{2,1,0:T(8,128)(2,1)S(1)}, bf16[1,64,128]{2,1,0:T(8,128)(2,1)S(1)}, u32[]{:S(2)}, u32[]{:S(2)}) collective-permute-start(bf16[1,64,128]{2,1,0:T(8,128)(2,1)S(1)} %get-tuple-element.49), channel_id=1, source_target_pairs={{0,2},{2,4},{4,6},{6,8},{8,10},{10,12},{12,14},{14,16},{16,18},{18... | collective-permute-start | bytes 49160 | tf_op jit(solution)/shard_map/ppermute | solution.py:27
  29.7 1.9 collective-permute-start.6
  31.8 3.4 %collective-permute-done.6 = bf16[1,64,128]{2,1,0:T(8,128)(2,1)S(1)} collective-permute-done((bf16[1,64,128]{2,1,0:T(8,128)(2,1)S(1)}, bf16[1,64,128]{2,1,0:T(8,128)(2,1)S(1)}, u32[]{:S(2)}, u32[]{:S(2)}) %collective-permute-start.6) | collective-permute-done | bytes 16416 | tf_op jit(solution)/shard_map/ppermute | solution.py:29
  35.3 3.1 %collective-permute-start.7 = (bf16[6,64,1]{2,1,0:T(8,128)(2,1)S(1)}, bf16[6,64,1]{2,1,0:T(8,128)(2,1)S(1)}, u32[]{:S(2)}, u32[]{:S(2)}) collective-permute-start(bf16[6,64,1]{2,1,0:T(8,128)(2,1)S(1)} %get-tuple-element.45), channel_id=1, source_target_pairs={{0,1},{2,3},{4,5},{6,7},{8,9},{10,11},{12,13},{14,15},{16,17},{18,... | collective-permute-start | bytes 2312 | tf_op jit(solution)/shard_map/ppermute | solution.py:27
  42.7 3.9 %collective-permute-done.8 = bf16[6,64,1]{2,1,0:T(8,128)(2,1)S(1)} collective-permute-done((bf16[6,64,1]{2,1,0:T(8,128)(2,1)S(1)}, bf16[6,64,1]{2,1,0:T(8,128)(2,1)S(1)}, u32[]{:S(2)}, u32[]{:S(2)}) %collective-permute-start.8) | collective-permute-done | bytes 800 | tf_op jit(solution)/shard_map/ppermute | solution.py:29
  47.3 3.3 %fusion.24 = bf16[8,8,8,128]{3,2,1,0:T(8,128)(2,1)S(1)} fusion(bf16[2048,1024]{1,0:T(8,128)(2,1)} %param.17, bf16[1,64,2048]{2,1,0:T(8,128)(2,1)S(1)} %multiply_convert_fusion), kind=kOutput, calls=%fused_computation.29 | convolution fusion | flops 268500992 | bytes 4587520 | tf_op jit(solution)/shard_map/dot_general | solution.py:182
  50.6 13.1 %all-gather.3.cloned.1.call-done = bf16[1024,1024]{1,0:T(8,128)(2,1)} async-done(((bf16[64,1024]{1,0:T(8,128)(2,1)}), bf16[1024,1024]{1,0:T(8,128)(2,1)}) %all-gather.3.cloned.1.call-update) | async-done | bytes 2097168 | tf_op jit(solution)/shard_map/all_gather | solution.py:187
  63.7 2.5 %multiply_reduce_fusion = (f32[8,64]{1,0:T(8,128)S(1)}, f32[8,64,1024]{2,1,0:T(8,128)S(1)}) fusion(bf16[8,8,8,128]{3,2,1,0:T(8,128)(2,1)S(1)} %fusion.24, bf16[1024,1024]{1,0:T(8,128)(2,1)} %all-gather.3.cloned.1.call-done), kind=kOutput, calls=%fused_computation.11 | convolution fusion | flops 135265792 | bytes 4327424 | tf_op jit(solution)/shard_map/qhd,khd->hqk/dot_general | solution.py:191
  66.3 1.3 copy-done.1
  68.1 38.6 %all-gather.5.cloned.1.call-done = bf16[1024,1024]{1,0:T(8,128)(2,1)} async-done(((bf16[64,1024]{1,0:T(8,128)(2,1)}), bf16[1024,1024]{1,0:T(8,128)(2,1)}) %all-gather.5.cloned.1.call-update) | async-done | bytes 2097168 | tf_op jit(solution)/shard_map/all_gather | solution.py:188
  106.7 3.2 %fusion.26 = bf16[8,8,8,128]{3,2,1,0:T(8,128)(2,1)S(1)} fusion(f32[8,64,1024]{2,1,0:T(8,128)} %copy-done.1, f32[8,64]{1,0:T(8,128)S(1)} %broadcast_maximum_fusion, f32[64,8]{0,1:T(8,128)S(1)} %bitcast.158, bf16[1024,1024]{1,0:T(8,128)(2,1)} %all-gather.5.cloned.1.call-done), kind=kOutput, calls=%fused_computation.33 | convolution fusion | flops 135921664 | bytes 4329472 | tf_op jit(solution)/shard_map/hqk,khd->hqd/dot_general | solution.py:197
  110.1 1.5 convolution_convert_fusion
  115.2 7.9 %reduce-scatter.2.cloned.1.call-done = bf16[32,2048]{1,0:T(8,128)(2,1)} async-done(((bf16[64,2048]{1,0:T(8,128)(2,1)}), bf16[32,2048]{1,0:T(8,128)(2,1)}) %reduce-scatter.2.cloned.1.call-update) | async-done | bytes 131088 | tf_op jit(solution)/shard_map/reduce_scatter | solution.py:206
  123.1 3.1 %convolution_convert_fusion.4 = bf16[32,1024]{1,0:T(8,128)(2,1)S(1)} fusion(bf16[2048,1024]{1,0:T(8,128)(2,1)} %param.21, bf16[32,2048]{1,0:T(8,128)(2,1)} %reduce-scatter.2.cloned.1.call-done, bf16[1,64,2048]{2,1,0:T(8,128)(2,1)S(1)} %multiply_convert_fusion, s32[]{:T(128)S(6)} %select_n.7), kind=kOutput, calls=%fused_computation.35 | convolution fusion | flops 134512640 | bytes 4521988 | tf_op jit(solution)/shard_map/dot_general | solution.py:213
  126.4 3.6 %collective-permute-start.1 = (bf16[2,64,128]{1,2,0:T(8,128)(2,1)S(1)}, bf16[2,64,128]{1,2,0:T(8,128)(2,1)S(1)}, u32[]{:S(2)}, u32[]{:S(2)}) collective-permute-start(bf16[2,64,128]{1,2,0:T(8,128)(2,1)S(1)} %bitcast.156), channel_id=1, source_target_pairs={{0,2},{2,4},{4,6},{6,8},{8,10},{10,12},{12,14},{14,16},{16,18},{18... | collective-permute-start | bytes 98312 | tf_op jit(solution)/shard_map/ppermute | solution.py:27
  130.1 1.9 collective-permute-start.2
  132.8 2.9 %collective-permute-done.2 = bf16[2,64,128]{1,2,0:T(8,128)(2,1)S(1)} collective-permute-done((bf16[2,64,128]{1,2,0:T(8,128)(2,1)S(1)}, bf16[2,64,128]{1,2,0:T(8,128)(2,1)S(1)}, u32[]{:S(2)}, u32[]{:S(2)}) %collective-permute-start.2) | collective-permute-done | bytes 32800 | tf_op jit(solution)/shard_map/ppermute | solution.py:29
  135.7 2.2 %collective-permute-start.3 = (bf16[8,64,2]{1,2,0:T(2,128)(2,1)S(1)}, bf16[8,64,2]{1,2,0:T(2,128)(2,1)S(1)}, u32[]{:S(2)}, u32[]{:S(2)}) collective-permute-start(bf16[8,64,2]{1,2,0:T(2,128)(2,1)S(1)} %get-tuple-element.35), channel_id=1, source_target_pairs={{0,1},{2,3},{4,5},{6,7},{8,9},{10,11},{12,13},{14,15},{16,17},{18,... | collective-permute-start | bytes 6152 | tf_op jit(solution)/shard_map/ppermute | solution.py:27
  139.9 2.3 %collective-permute-done.4 = bf16[8,64,2]{1,2,0:T(2,128)(2,1)S(1)} collective-permute-done((bf16[8,64,2]{1,2,0:T(2,128)(2,1)S(1)}, bf16[8,64,2]{1,2,0:T(2,128)(2,1)S(1)}, u32[]{:S(2)}, u32[]{:S(2)}) %collective-permute-start.4) | collective-permute-done | bytes 2080 | tf_op jit(solution)/shard_map/ppermute | solution.py:29
  145.2 3.3 %concatenate.94 = bf16[6,576,130]{1,2,0:T(8,128)(2,1)} concatenate(bf16[6,64,130]{1,2,0:T(8,128)(2,1)S(1)} %get-tuple-element.59, bf16[6,64,130]{1,2,0:T(8,128)(2,1)} %get-tuple-element.28, bf16[6,64,130]{1,2,0:T(8,128)(2,1)S(1)} %get-tuple-element.25, bf16[6,64,130]{1,2,0:T(8,128)(2,1)S(1)} %get-tuple-element.60, bf16[6,64,130]{1,2,0:T(8,128)(2,1)} %get-tuple-element.27, ...), dimensions={1} | concatenate | bytes 1797120 | tf_op jit(solution)/shard_map/concatenate | solution.py:42
  148.5 1.9 fusion.41
  150.4 1.5 convert_reduce_fusion
  151.9 1.4 concatenate.110
  156.7 25.6 %shard_map.164 = f32[32,24,128]{2,1,0:T(8,128)S(1)} custom-call(f32[32,24,128]{2,1,0:T(8,128)S(1)} %bitcast.140), custom_call_target="tpu_custom_call" | custom-call | tf_op jit(solution)/shard_map/pallas_call | solution.py:141
  182.3 2.1 %collective-permute-start.10 = (bf16[1,64,128]{2,1,0:T(8,128)(2,1)S(1)}, bf16[1,64,128]{2,1,0:T(8,128)(2,1)S(1)}, u32[]{:S(2)}, u32[]{:S(2)}) collective-permute-start(bf16[1,64,128]{2,1,0:T(8,128)(2,1)S(1)} %get-tuple-element.47), channel_id=1, source_target_pairs={{2,0},{4,2},{6,4},{8,6},{10,8},{12,10},{14,12},{16,14},{18,16},{20... | collective-permute-start | bytes 49160 | tf_op jit(solution)/shard_map/ppermute | solution.py:29
  184.4 3.5 %collective-permute-start.9 = (bf16[1,64,128]{2,1,0:T(8,128)(2,1)S(1)}, bf16[1,64,128]{2,1,0:T(8,128)(2,1)S(1)}, u32[]{:S(2)}, u32[]{:S(2)}) collective-permute-start(bf16[1,64,128]{2,1,0:T(8,128)(2,1)S(1)} %get-tuple-element.46), channel_id=1, source_target_pairs={{0,2},{2,4},{4,6},{6,8},{8,10},{10,12},{12,14},{14,16},{16,18},{18... | collective-permute-start | bytes 49160 | tf_op jit(solution)/shard_map/ppermute | solution.py:27
  190.2 3.2 %collective-permute-start.11 = (bf16[6,64,1]{2,1,0:T(8,128)(2,1)S(1)}, bf16[6,64,1]{2,1,0:T(8,128)(2,1)S(1)}, u32[]{:S(2)}, u32[]{:S(2)}) collective-permute-start(bf16[6,64,1]{2,1,0:T(8,128)(2,1)S(1)} %get-tuple-element.43), channel_id=1, source_target_pairs={{0,1},{2,3},{4,5},{6,7},{8,9},{10,11},{12,13},{14,15},{16,17},{18,... | collective-permute-start | bytes 2312 | tf_op jit(solution)/shard_map/ppermute | solution.py:27
  196.0 3.1 %collective-permute-done.12 = bf16[6,64,1]{2,1,0:T(8,128)(2,1)S(1)} collective-permute-done((bf16[6,64,1]{2,1,0:T(8,128)(2,1)S(1)}, bf16[6,64,1]{2,1,0:T(8,128)(2,1)S(1)}, u32[]{:S(2)}, u32[]{:S(2)}) %collective-permute-start.12) | collective-permute-done | bytes 800 | tf_op jit(solution)/shard_map/ppermute | solution.py:29
  (114 shorter events, 28.2 us)
Async XLA Ops:
  7.2 2.2 %copy-start = (bf16[8,64,2048]{2,1,0:T(8,128)(2,1)S(1)}, bf16[8,64,2048]{2,1,0:T(8,128)(2,1)}, u32[]{:S(2)}) copy-start(bf16[8,64,2048]{2,1,0:T(8,128)(2,1)} %param.14) | copy-start | bytes 6291460
  7.2 10.1 %copy-start.9 = (f32[2048]{0:T(1024)S(1)}, f32[2048]{0:T(1024)}, u32[]{:S(2)}) copy-start(f32[2048]{0:T(1024)} %param.16) | copy-start | bytes 24580
  7.2 56.5 %all-gather.3.cloned.1.call-start = ((), (), s32[]{:S(2)}) async-start(), calls=%async_computation.1 | async-start | bytes 2228224 | tf_op jit(solution)/shard_map/all_gather | solution.py:187
  9.9 7.2 %collective-permute-start = (bf16[1,64,2048]{2,1,0:T(8,128)(2,1)S(1)}, bf16[1,64,2048]{2,1,0:T(8,128)(2,1)S(1)}, u32[]{:S(2)}, u32[]{:S(2)}) collective-permute-start(bf16[1,64,2048]{2,1,0:T(8,128)(2,1)S(1)} %fusion.1), channel_id=1, source_target_pairs={{0,1},{1,0},{2,3},{3,2},{4,5},{5,4},{6,7},{7,6},{8,9},{9,8},{10,11... | collective-permute-start | bytes 786440 | tf_op jit(solution)/shard_map/ppermute | solution.py:171
  21.2 3.9 %copy-start.3 = (bf16[4,64,128]{2,1,0:T(8,128)(2,1)S(1)}, bf16[4,64,128]{2,1,0:T(8,128)(2,1)}, u32[]{:S(2)}) copy-start(bf16[4,64,128]{2,1,0:T(8,128)(2,1)} %param.25) | copy-start | bytes 196612
  21.2 10.5 %copy-start.4 = (bf16[9,64,64]{2,1,0:T(8,128)(2,1)S(1)}, bf16[9,64,64]{2,1,0:T(8,128)(2,1)}, u32[]{:S(2)}) copy-start(bf16[9,64,64]{2,1,0:T(8,128)(2,1)} %param.24) | copy-start | bytes 221188
  21.2 17.2 %copy-start.7 = (bf16[9,64,64]{2,1,0:T(8,128)(2,1)S(1)}, bf16[9,64,64]{2,1,0:T(8,128)(2,1)}, u32[]{:S(2)}) copy-start(bf16[9,64,64]{2,1,0:T(8,128)(2,1)} %param.22) | copy-start | bytes 221188
  21.2 85.5 %all-gather.5.cloned.1.call-start = ((), (), s32[]{:S(2)}) async-start(), calls=%async_computation.2 | async-start | bytes 2228224 | tf_op jit(solution)/shard_map/all_gather | solution.py:188
  25.1 98.0 %reduce-scatter.2.cloned.1.call-start = ((), (), s32[]{:S(2)}) async-start(), calls=%async_computation.3 | async-start | bytes 393216 | tf_op jit(solution)/shard_map/reduce_scatter | solution.py:206
  25.1 6.6 %collective-permute-start.5 = (bf16[1,64,128]{2,1,0:T(8,128)(2,1)S(1)}, bf16[1,64,128]{2,1,0:T(8,128)(2,1)S(1)}, u32[]{:S(2)}, u32[]{:S(2)}) collective-permute-start(bf16[1,64,128]{2,1,0:T(8,128)(2,1)S(1)} %get-tuple-element.49), channel_id=1, source_target_pairs={{0,2},{2,4},{4,6},{6,8},{8,10},{10,12},{12,14},{14,16},{16,18},{18... | collective-permute-start | bytes 49160 | tf_op jit(solution)/shard_map/ppermute | solution.py:27
  29.7 5.5 %collective-permute-start.6 = (bf16[1,64,128]{2,1,0:T(8,128)(2,1)S(1)}, bf16[1,64,128]{2,1,0:T(8,128)(2,1)S(1)}, u32[]{:S(2)}, u32[]{:S(2)}) collective-permute-start(bf16[1,64,128]{2,1,0:T(8,128)(2,1)S(1)} %get-tuple-element.48), channel_id=1, source_target_pairs={{2,0},{4,2},{6,4},{8,6},{10,8},{12,10},{14,12},{16,14},{18,16},{20... | collective-permute-start | bytes 49160 | tf_op jit(solution)/shard_map/ppermute | solution.py:29
  35.3 6.0 %collective-permute-start.7 = (bf16[6,64,1]{2,1,0:T(8,128)(2,1)S(1)}, bf16[6,64,1]{2,1,0:T(8,128)(2,1)S(1)}, u32[]{:S(2)}, u32[]{:S(2)}) collective-permute-start(bf16[6,64,1]{2,1,0:T(8,128)(2,1)S(1)} %get-tuple-element.45), channel_id=1, source_target_pairs={{0,1},{2,3},{4,5},{6,7},{8,9},{10,11},{12,13},{14,15},{16,17},{18,... | collective-permute-start | bytes 2312 | tf_op jit(solution)/shard_map/ppermute | solution.py:27
  40.0 6.5 %collective-permute-start.8 = (bf16[6,64,1]{2,1,0:T(8,128)(2,1)S(1)}, bf16[6,64,1]{2,1,0:T(8,128)(2,1)S(1)}, u32[]{:S(2)}, u32[]{:S(2)}) collective-permute-start(bf16[6,64,1]{2,1,0:T(8,128)(2,1)S(1)} %get-tuple-element.44), channel_id=1, source_target_pairs={{1,0},{3,2},{5,4},{7,6},{9,8},{11,10},{13,12},{15,14},{17,16},{19,... | collective-permute-start | bytes 2312 | tf_op jit(solution)/shard_map/ppermute | solution.py:29
  66.2 1.3 copy-start.1
  106.7 3.4 %copy-start.2 = (bf16[1024,2048]{1,0:T(8,128)(2,1)S(1)}, bf16[1024,2048]{1,0:T(8,128)(2,1)}, u32[]{:S(2)}) copy-start(bf16[1024,2048]{1,0:T(8,128)(2,1)} %param.20) | copy-start | bytes 12582916
  126.4 6.4 %collective-permute-start.1 = (bf16[2,64,128]{1,2,0:T(8,128)(2,1)S(1)}, bf16[2,64,128]{1,2,0:T(8,128)(2,1)S(1)}, u32[]{:S(2)}, u32[]{:S(2)}) collective-permute-start(bf16[2,64,128]{1,2,0:T(8,128)(2,1)S(1)} %bitcast.156), channel_id=1, source_target_pairs={{0,2},{2,4},{4,6},{6,8},{8,10},{10,12},{12,14},{14,16},{16,18},{18... | collective-permute-start | bytes 98312 | tf_op jit(solution)/shard_map/ppermute | solution.py:27
  130.1 5.6 %collective-permute-start.2 = (bf16[2,64,128]{1,2,0:T(8,128)(2,1)S(1)}, bf16[2,64,128]{1,2,0:T(8,128)(2,1)S(1)}, u32[]{:S(2)}, u32[]{:S(2)}) collective-permute-start(bf16[2,64,128]{1,2,0:T(8,128)(2,1)S(1)} %bitcast.157), channel_id=1, source_target_pairs={{2,0},{4,2},{6,4},{8,6},{10,8},{12,10},{14,12},{16,14},{18,16},{20... | collective-permute-start | bytes 98312 | tf_op jit(solution)/shard_map/ppermute | solution.py:29
  135.7 4.2 %collective-permute-start.3 = (bf16[8,64,2]{1,2,0:T(2,128)(2,1)S(1)}, bf16[8,64,2]{1,2,0:T(2,128)(2,1)S(1)}, u32[]{:S(2)}, u32[]{:S(2)}) collective-permute-start(bf16[8,64,2]{1,2,0:T(2,128)(2,1)S(1)} %get-tuple-element.35), channel_id=1, source_target_pairs={{0,1},{2,3},{4,5},{6,7},{8,9},{10,11},{12,13},{14,15},{16,17},{18,... | collective-permute-start | bytes 6152 | tf_op jit(solution)/shard_map/ppermute | solution.py:27
  137.9 4.4 %collective-permute-start.4 = (bf16[8,64,2]{1,2,0:T(2,128)(2,1)S(1)}, bf16[8,64,2]{1,2,0:T(2,128)(2,1)S(1)}, u32[]{:S(2)}, u32[]{:S(2)}) collective-permute-start(bf16[8,64,2]{1,2,0:T(2,128)(2,1)S(1)} %get-tuple-element.34), channel_id=1, source_target_pairs={{1,0},{3,2},{5,4},{7,6},{9,8},{11,10},{13,12},{15,14},{17,16},{19,... | collective-permute-start | bytes 6152 | tf_op jit(solution)/shard_map/ppermute | solution.py:29
  144.3 4.2 %copy-start.10 = (f32[64]{0:T(128)S(1)}, f32[64]{0:T(128)}, u32[]{:S(2)}) copy-start(f32[64]{0:T(128)} %param.23) | copy-start | bytes 772
  148.5 1.9 copy-start.8
  148.5 3.4 %copy-start.6 = (bf16[4,64,128]{1,2,0:T(8,128)(2,1)S(1)}, bf16[4,64,128]{1,2,0:T(8,128)(2,1)}, u32[]{:S(2)}) copy-start(bf16[4,64,128]{1,2,0:T(8,128)(2,1)} %get-tuple-element.18) | copy-start | bytes 196612
  182.3 7.8 %collective-permute-start.10 = (bf16[1,64,128]{2,1,0:T(8,128)(2,1)S(1)}, bf16[1,64,128]{2,1,0:T(8,128)(2,1)S(1)}, u32[]{:S(2)}, u32[]{:S(2)}) collective-permute-start(bf16[1,64,128]{2,1,0:T(8,128)(2,1)S(1)} %get-tuple-element.47), channel_id=1, source_target_pairs={{2,0},{4,2},{6,4},{8,6},{10,8},{12,10},{14,12},{16,14},{18,16},{20... | collective-permute-start | bytes 49160 | tf_op jit(solution)/shard_map/ppermute | solution.py:29
  184.4 5.7 %collective-permute-start.9 = (bf16[1,64,128]{2,1,0:T(8,128)(2,1)S(1)}, bf16[1,64,128]{2,1,0:T(8,128)(2,1)S(1)}, u32[]{:S(2)}, u32[]{:S(2)}) collective-permute-start(bf16[1,64,128]{2,1,0:T(8,128)(2,1)S(1)} %get-tuple-element.46), channel_id=1, source_target_pairs={{0,2},{2,4},{4,6},{6,8},{8,10},{10,12},{12,14},{14,16},{16,18},{18... | collective-permute-start | bytes 49160 | tf_op jit(solution)/shard_map/ppermute | solution.py:27
  189.2 10.5 %copy-start.5 = (bf16[9,64,64]{2,1,0:T(8,128)(2,1)S(1)}, bf16[9,64,64]{2,1,0:T(8,128)(2,1)}, u32[]{:S(2)}) copy-start(bf16[9,64,64]{2,1,0:T(8,128)(2,1)} %copy.44) | copy-start | bytes 221188
  190.2 5.8 %collective-permute-start.11 = (bf16[6,64,1]{2,1,0:T(8,128)(2,1)S(1)}, bf16[6,64,1]{2,1,0:T(8,128)(2,1)S(1)}, u32[]{:S(2)}, u32[]{:S(2)}) collective-permute-start(bf16[6,64,1]{2,1,0:T(8,128)(2,1)S(1)} %get-tuple-element.43), channel_id=1, source_target_pairs={{0,1},{2,3},{4,5},{6,7},{8,9},{10,11},{12,13},{14,15},{16,17},{18,... | collective-permute-start | bytes 2312 | tf_op jit(solution)/shard_map/ppermute | solution.py:27
  193.4 5.7 %collective-permute-start.12 = (bf16[6,64,1]{2,1,0:T(8,128)(2,1)S(1)}, bf16[6,64,1]{2,1,0:T(8,128)(2,1)S(1)}, u32[]{:S(2)}, u32[]{:S(2)}) collective-permute-start(bf16[6,64,1]{2,1,0:T(8,128)(2,1)S(1)} %get-tuple-element.42), channel_id=1, source_target_pairs={{1,0},{3,2},{5,4},{7,6},{9,8},{11,10},{13,12},{15,14},{17,16},{19,... | collective-permute-start | bytes 2312 | tf_op jit(solution)/shard_map/ppermute | solution.py:29
Sparse Core Ops, SparseCore 0:
  21.3 42.3 all-gather.2
  66.4 40.1 all-gather.4
  111.8 11.2 reduce-scatter.1

commit v2 on v1

--- a/solution.py
+++ b/solution.py
@@ -60,12 +60,6 @@
     stacked = tap_stack(padded, grads.shape[0], grads.shape[2])
     summed = jnp.einsum("ykx,yox->ko", stacked, grads, preferred_element_type=jnp.float32)
     return summed.reshape(9, padded.shape[1], grads.shape[1])
-
-
-def normalize(mixed, agg_gain):
-    return (
-        mixed * lax.rsqrt(jnp.mean(mixed * mixed, axis=-1, keepdims=True) + 1e-05) * agg_gain
-    ).astype(jnp.bfloat16)
 
 
 def gradient_rim(field):
@@ -152,6 +146,269 @@
     return summed.reshape(rows * count, terms.shape[1])
 
 
+def token_kernel(
+    bands, heads, parts,
+    mix_ref, gain_ref, wq_any, wk_any, wv_any, wo_any, up_any,
+    o_ref,
+    wq, wk, wv, wo, up, mixes, normed, query, key, value, query_all, key_all, value_all,
+    context, joined, partial, slabs,
+    load, mix_out, mix_in, key_out, key_in, value_out, value_in, query_out, query_in,
+    context_out, context_in, slab_out, slab_in,
+):
+    band = lax.axis_index("band")
+    var = lax.axis_index("var")
+    rows = mix_ref.shape[0]
+    slab_rows = rows // parts
+    head = lax.rem(band, heads)
+    first = band - head
+
+    def columns(index):
+        return pl.ds(pl.multiple_of(index * HD, HD), HD)
+
+    def lines(index, size):
+        return pl.ds(pl.multiple_of(index * size, size), size)
+
+    def remote(src, dst, out_sem, in_sem, to_band, to_var):
+        return pltpu.make_async_remote_copy(
+            src_ref=src, dst_ref=dst, send_sem=out_sem, recv_sem=in_sem,
+            device_id=(to_band, to_var), device_id_type=MESH,
+        )
+
+    def other_band(step):
+        return lax.rem(band + step, bands)
+
+    def other_head(step):
+        return lax.rem(head + step, heads)
+
+    def other_var(step):
+        return lax.rem(var + step, parts)
+
+    def send_mix(step):
+        return remote(
+            mix_ref, mixes.at[step], mix_out.at[step], mix_in.at[step], band, other_var(step)
+        )
+
+    def send_rows(source, target, out_sem, in_sem, step):
+        peer = other_band(step)
+        return remote(
+            source.at[:, columns(lax.rem(peer, heads))],
+            target.at[lines(band, rows)],
+            out_sem.at[step], in_sem.at[step], peer, var,
+        )
+
+    def send_query(step):
+        peer = other_head(step)
+        return remote(
+            query.at[:, columns(peer)],
+            query_all.at[lines(head, rows)],
+            query_out.at[step], query_in.at[step], first + peer, var,
+        )
+
+    def send_context(peer):
+        return remote(
+            context.at[lines(peer, rows)],
+            joined.at[:, columns(head)],
+            context_out.at[peer], context_in.at[head], first + peer, var,
+        )
+
+    def take_context(owner):
+        return remote(
+            context.at[lines(owner, rows)],
+            joined.at[:, columns(owner)],
+            context_out.at[owner], context_in.at[owner], first + owner, var,
+        )
+
+    def send_slab(step):
+        peer = other_var(step)
+        return remote(
+            partial.at[lines(peer, slab_rows)],
+            slabs.at[step],
+            slab_out.at[step], slab_in.at[step], band, peer,
+        )
+
+    barrier = pltpu.get_barrier_semaphore()
+
+    @pl.loop(1, parts)
+    def _(step):
+        pl.semaphore_signal(
+            barrier, inc=1, device_id=(band, other_var(step)), device_id_type=MESH
+        )
+
+    @pl.loop(1, bands)
+    def _(step):
+        pl.semaphore_signal(
+            barrier, inc=1, device_id=(other_band(step), var), device_id_type=MESH
+        )
+
+    loads = [
+        pltpu.make_async_copy(source, target, load.at[index])
+        for index, (source, target) in enumerate(
+            ((wk_any, wk), (wq_any, wq), (wv_any, wv), (wo_any, wo), (up_any, up))
+        )
+    ]
+    for item in loads:
+        item.start()
+    pl.semaphore_wait(barrier, bands + parts - 2)
+    for step in range(1, parts):
+        send_mix(step).start()
+    mixed = mix_ref[...].astype(jnp.float32)
+    for step in range(1, parts):
+        send_mix(step).wait_recv()
+        mixed = mixed + mixes[step].astype(jnp.float32)
+    scale = lax.rsqrt(jnp.mean(mixed * mixed, axis=-1, keepdims=True) + 1e-05)
+    normed[...] = (mixed * scale * gain_ref[...]).astype(jnp.bfloat16)
+
+    def project(weight):
+        return jnp.dot(
+            normed[...], weight[...], preferred_element_type=jnp.float32
+        ).astype(jnp.bfloat16)
+
+    loads[0].wait()
+    key[...] = project(wk)
+
+    @pl.loop(1, bands)
+    def _(step):
+        send_rows(key, key_all, key_out, key_in, step).start()
+
+    loads[1].wait()
+    query[...] = project(wq)
+
+    @pl.loop(1, heads)
+    def _(step):
+        send_query(step).start()
+
+    loads[2].wait()
+    value[...] = project(wv)
+
+    @pl.loop(1, bands)
+    def _(step):
+        send_rows(value, value_all, value_out, value_in, step).start()
+
+    key_all[lines(band, rows), :] = key[:, columns(head)]
+    value_all[lines(band, rows), :] = value[:, columns(head)]
+    query_all[lines(head, rows), :] = query[:, columns(head)]
+
+    def arrived(source, target, out_sem, in_sem, step):
+        peer = lax.rem(band - step + bands, bands)
+        return remote(
+            source.at[:, columns(head)],
+            target.at[lines(peer, rows)],
+            out_sem.at[step], in_sem.at[step], other_band(step), var,
+        )
+
+    def arrived_query(step):
+        peer = lax.rem(head - step + heads, heads)
+        return remote(
+            query.at[:, columns(head)],
+            query_all.at[lines(peer, rows)],
+            query_out.at[step], query_in.at[step], first + other_head(step), var,
+        )
+
+    @pl.loop(1, bands)
+    def _(step):
+        arrived(key, key_all, key_out, key_in, step).wait_recv()
+
+    @pl.loop(1, heads)
+    def _(step):
+        arrived_query(step).wait_recv()
+
+    group = max(1, min(heads, 256 // rows))
+    size = group * rows
+    for index in range(heads // group):
+        scores = lax.dot_general(
+            query_all[index * size : (index + 1) * size, :],
+            key_all[...],
+            (((1,), (1,)), ((), ())),
+            preferred_element_type=jnp.float32,
+        ) * (1.0 / math.sqrt(HD))
+        weights = jnp.exp(scores - jnp.max(scores, axis=1, keepdims=True))
+        total = jnp.sum(weights, axis=1, keepdims=True)
+        probs = weights.astype(jnp.bfloat16)
+        if index == 0:
+
+            @pl.loop(1, bands)
+            def _(step):
+                arrived(value, value_all, value_out, value_in, step).wait_recv()
+
+        update = jnp.dot(probs, value_all[...], preferred_element_type=jnp.float32)
+        context[index * size : (index + 1) * size, :] = (update / total).astype(jnp.bfloat16)
+
+        @pl.loop(index * group, (index + 1) * group)
+        def _(peer):
+            @pl.when(peer != head)
+            def _():
+                send_context(peer).start()
+
+    joined[:, columns(head)] = context[lines(head, rows), :]
+    loads[3].wait()
+    loads[4].wait()
+
+    @pl.loop(1, heads)
+    def _(step):
+        take_context(other_head(step)).wait_recv()
+
+    partial[...] = jnp.dot(
+        joined[...], wo[...], preferred_element_type=jnp.float32
+    ).astype(jnp.bfloat16)
+    for step in range(1, parts):
+        send_slab(step).start()
+    hidden = partial[lines(var, slab_rows), :].astype(jnp.float32)
+    for step in range(1, parts):
+        send_slab(step).wait_recv()
+        hidden = hidden + slabs[step].astype(jnp.float32)
+    hidden = (hidden + normed[lines(var, slab_rows), :].astype(jnp.float32)).astype(jnp.bfloat16)
+    o_ref[...] = jnp.dot(hidden, up[...], preferred_element_type=jnp.float32).astype(jnp.bfloat16)
+
+    for step in range(1, parts):
+        send_mix(step).wait_send()
+        send_slab(step).wait_send()
+
+    @pl.loop(1, bands)
+    def _(step):
+        send_rows(key, key_all, key_out, key_in, step).wait_send()
+        send_rows(value, value_all, value_out, value_in, step).wait_send()
+
+    @pl.loop(1, heads)
+    def _(step):
+        send_query(step).wait_send()
+        send_context(other_head(step)).wait_send()
+
+
+def token_stage(own_mix, agg_gain, wq, wk, wv, wo, w_up, bands, parts):
+    rows = own_mix.shape[0]
+    wide = wq.shape[1]
+    heads = wide // HD
+    fine = w_up.shape[1]
+
+    def half(*shape):
+        return pltpu.VMEM(shape, jnp.bfloat16)
+
+    def flags(count):
+        return pltpu.SemaphoreType.DMA((count,))
+
+    vmem = pl.BlockSpec(memory_space=pltpu.VMEM)
+    return pl.pallas_call(
+        functools.partial(token_kernel, bands, heads, parts),
+        out_shape=jax.ShapeDtypeStruct((rows // parts, fine), jnp.bfloat16),
+        in_specs=[vmem, vmem] + [pl.BlockSpec(memory_space=pl.ANY)] * 5,
+        out_specs=vmem,
+        scratch_shapes=[
+            half(D, wide), half(D, wide), half(D, wide), half(wide, D), half(D, fine),
+            half(parts, rows, D), half(rows, D),
+            half(rows, wide), half(rows, wide), half(rows, wide),
+            half(heads * rows, HD), half(bands * rows, HD), half(bands * rows, HD),
+            half(heads * rows, HD), half(rows, wide), half(rows, D),
+            half(parts, rows // parts, D),
+            flags(5), flags(parts), flags(parts), flags(bands), flags(bands), flags(bands),
+            flags(bands), flags(heads), flags(heads), flags(heads), flags(heads),
+            flags(parts), flags(parts),
+        ],
+        compiler_params=pltpu.CompilerParams(
+            collective_id=1, has_side_effects=True, vmem_limit_bytes=56 << 20
+        ),
+    )(own_mix, agg_gain[None], wq, wk, wv, wo, w_up)
+
+
 def on_device(
     patches, w_embed, var_bias, agg_gain, wq, wk, wv, wo, w_up, conv1, bias1, conv2, cotangent
 ):
@@ -165,52 +422,13 @@
     partial_mix = jnp.dot(
         flattened, w_embed.reshape(var_local * patch_len, D), preferred_element_type=jnp.float32
     )
-    partial_mix = (partial_mix + jnp.sum(var_bias, axis=0)).reshape(lat_dev, lon_all, D)
-    own_mix = partial_mix.astype(jnp.bfloat16)
-    if var_count == 2:
-        other_mix = lax.ppermute(own_mix, "var", [(0, 1), (1, 0)])
-        mixed = own_mix.astype(jnp.float32) + other_mix.astype(jnp.float32)
-    else:
-        mixed = lax.psum(own_mix, "var").astype(jnp.float32)
-    normed_band = normalize(mixed, agg_gain)
-    normed_slab = lax.dynamic_slice_in_dim(normed_band, lax.axis_index("var") * lon_dev, lon_dev, 1)
+    own_mix = (partial_mix + jnp.sum(var_bias, axis=0)).astype(jnp.bfloat16)
     token_rows = jnp.transpose(
-        normed_band.reshape(lat_dev, var_count, lon_dev, D), (1, 0, 2, 3)
+        own_mix.reshape(lat_dev, var_count, lon_dev, D), (1, 0, 2, 3)
     ).reshape(-1, D)
-    heads_local = wq.shape[1] // HD
-    query_rows = token_rows.shape[0]
-    queries = jnp.dot(token_rows, wq, preferred_element_type=jnp.float32).astype(jnp.bfloat16)
-    keys_local = jnp.dot(token_rows, wk, preferred_element_type=jnp.float32).astype(jnp.bfloat16)
-    values_local = jnp.dot(token_rows, wv, preferred_element_type=jnp.float32).astype(jnp.bfloat16)
-    query_heads = queries.reshape(query_rows, heads_local, HD)
-    running_max = jnp.full((heads_local, query_rows), -1e30, jnp.float32)
-    key_heads = lax.all_gather(keys_local, "band", axis=0, tiled=True).reshape(-1, heads_local, HD)
-    value_heads = lax.all_gather(values_local, "band", axis=0, tiled=True).reshape(
-        -1, heads_local, HD
-    )
-    scores = jnp.einsum(
-        "qhd,khd->hqk", query_heads, key_heads, preferred_element_type=jnp.float32
-    ) / math.sqrt(HD)
-    new_max = jnp.maximum(running_max, jnp.max(scores, axis=2))
-    weights = jnp.exp(scores - new_max[:, :, None])
-    new_sum = jnp.sum(weights, axis=2)
-    update = jnp.einsum(
-        "hqk,khd->hqd",
-        weights.astype(jnp.bfloat16),
-        value_heads,
-        preferred_element_type=jnp.float32,
-    )
-    context = (update / new_sum[:, :, None]).astype(jnp.bfloat16)
-    context = jnp.transpose(context, (1, 0, 2)).reshape(query_rows, heads_local * HD)
-    slab_rows = lat_dev * lon_dev
-    attended = lax.psum_scatter(
-        jnp.dot(context, wo, preferred_element_type=jnp.float32).astype(jnp.bfloat16),
-        "var",
-        scatter_dimension=0,
-        tiled=True,
-    ).astype(jnp.float32)
-    hidden = (normed_slab.reshape(slab_rows, D).astype(jnp.float32) + attended).astype(jnp.bfloat16)
-    upsampled = jnp.dot(hidden, w_up, preferred_element_type=jnp.float32).astype(jnp.bfloat16)
+    upsampled = token_stage(
+        token_rows, agg_gain, wq, wk, wv, wo, w_up, band_count, var_count
+    )
     height = lat_dev * R
     width = lon_dev * R
     upsampled = jnp.transpose(

time: 209 us -> 140 us (0.67)
  waiting for transfers between devices: 81.2 us -> 11.1 us
  Pallas kernels: 25.6 us -> 66.3 us
  matrix products: 27.7 us -> 8.87 us
  between operations: 14.3 us -> 1.13 us
  other arithmetic: 8.72 us -> 4.4 us
  starting transfers between devices: 31.4 us -> 28.2 us
    all_gather x2 -> x0, waiting for transfers between devices: 51.7 us -> none  [the longest x1 38.6 us: on_device(): lax.all_gather(values_local, 'band', axis=0, tiled=True)]
    pallas_call x0 -> x1, Pallas kernels: none -> 37.3 us  [token_stage(): pl.pallas_call(functools.partial(token_kernel, bands, heads, parts), out_...]
    dot_general x7 -> x0, matrix products: 21.1 us -> none  [the longest x1 3.78 us: on_device(): jnp.dot(token_rows, wv, preferred_element_type=jnp.float32)]
    reduce_scatter x1 -> x0, waiting for transfers between devices: 7.92 us -> none  [on_device(): lax.psum_scatter(jnp.dot(context, wo, preferred_element_type=jnp.float32)...]
    ppermute x1 -> x0, waiting for transfers between devices: 5.93 us -> none  [on_device(): other_mix = lax.ppermute(own_mix, 'var', [(0, 1), (1, 0)])]
    ppermute x6, waiting for transfers between devices: 15.5 us -> 11.1 us  [with_halo(): lax.ppermute(head, axis, [((i + 1) % count, i) for i in range(ends)])]
    unnamed x9, other arithmetic: 4.98 us -> 0.61 us
    pallas_call x1, Pallas kernels: 25.6 us -> 29 us  [sum_everywhere(): pl.pallas_call(functools.partial(sum_kernel, count, var_count), out_shape...]
  transfers between devices with their start and end apart: 16 -> 12, of which waited for: 9 -> 5; matrix products, arithmetic and copies ran while one was open for 11% -> 5% of each run, Pallas kernels for 0% -> 0%
where the time goes in v2:
time: 140 us; the launch traced here: 138 us
  Pallas kernels  66.3 us (47%)
  starting transfers between devices  28.2 us (20%)
  local copies, waits for them, and re-layouts  17.6 us (13%)
  waiting for transfers between devices  11.1 us (8%)
  matrix products  8.87 us (6%)
  other arithmetic  4.4 us (3%)
    pallas_call x1, Pallas kernels, token_stage(): pl.pallas_call(functools.partial(token_kernel, bands, heads, parts), out_...  37.3 us
    pallas_call x1, Pallas kernels, sum_everywhere(): pl.pallas_call(functools.partial(sum_kernel, count, var_count), out_shape...  29 us
    ppermute x6, starting transfers between devices, with_halo(): lax.ppermute(tail, axis, [(i, (i + 1) % count) for i in range(ends)])  17 us
    ppermute x6, starting transfers between devices, with_halo(): lax.ppermute(head, axis, [((i + 1) % count, i) for i in range(ends)])  11.2 us
    ppermute x6, waiting for transfers between devices, with_halo(): lax.ppermute(head, axis, [((i + 1) % count, i) for i in range(ends)])  11.1 us
    dot_general x4, matrix products, conv_padded(): jnp.einsum('ykx,ko->yox', stacked, weight.reshape(-1, weight.shape[2]), p...  6.47 us
    concatenate x4, local copies, waits for them, and re-layouts, tap_stack(): return jnp.concatenate(pieces, axis=1)  4.94 us
  transfers between devices with their start and end apart: 12, of which 5 were waited for; matrix products, arithmetic and copies ran while one was open for 5% of the time, Pallas kernels for 0%

profile of v2, /device:TPU:25, one launch (start us, length us, event | category | flops | bytes accessed | tf_op | source)
XLA Modules:
  0.0 137.6 jit_solution(8008270704666924194)
XLA Ops:
  0.6 1.1 copy.28
  2.8 1.2 fusion.mix_ref
  4.0 37.3 %shard_map.164 = bf16[32,1024]{1,0:T(8,128)(2,1)} custom-call(bf16[64,2048]{1,0:T(8,128)(2,1)} %fusion.mix_ref, f32[1,2048]{1,0:T(1,128)} %bitcast.94, bf16[2048,1024]{1,0:T(8,128)(2,1)} %wq_any.1, bf16[2048,1024]{1,0:T(8,128)(2,1)} %wk_any.1, bf16[2048,1024]{1,0:T(8,128)(2,1)} %wv_any.1, bf16[1024,2048]{1,0:T(8,128)(2,1)} %wo_any.1, bf16[2048,1024]{1,0:T(8,128)(2,1)} %up_any.1), custom_call_target="tpu_custom_call" | custom-call | tf_op jit(solution)/shard_map/pallas_call | solution.py:390
  41.3 1.0 reshape.98
  42.4 2.5 %collective-permute-start = (bf16[2,64,128]{1,2,0:T(8,128)(2,1)S(1)}, bf16[2,64,128]{1,2,0:T(8,128)(2,1)S(1)}, u32[]{:S(2)}, u32[]{:S(2)}) collective-permute-start(bf16[2,64,128]{1,2,0:T(8,128)(2,1)S(1)} %bitcast.92), channel_id=1, source_target_pairs={{0,2},{2,4},{4,6},{6,8},{8,10},{10,12},{12,14},{14,16},{16,18},{18... | collective-permute-start | bytes 98312 | tf_op jit(solution)/shard_map/ppermute | solution.py:27
  44.9 2.3 %collective-permute-start.1 = (bf16[2,64,128]{1,2,0:T(8,128)(2,1)S(1)}, bf16[2,64,128]{1,2,0:T(8,128)(2,1)S(1)}, u32[]{:S(2)}, u32[]{:S(2)}) collective-permute-start(bf16[2,64,128]{1,2,0:T(8,128)(2,1)S(1)} %bitcast.93), channel_id=1, source_target_pairs={{2,0},{4,2},{6,4},{8,6},{10,8},{12,10},{14,12},{16,14},{18,16},{20... | collective-permute-start | bytes 98312 | tf_op jit(solution)/shard_map/ppermute | solution.py:29
  47.2 3.3 %collective-permute-start.4 = (bf16[1,64,128]{2,1,0:T(8,128)(2,1)S(1)}, bf16[1,64,128]{2,1,0:T(8,128)(2,1)S(1)}, u32[]{:S(2)}, u32[]{:S(2)}) collective-permute-start(bf16[1,64,128]{2,1,0:T(8,128)(2,1)S(1)} %get-tuple-element.49), channel_id=1, source_target_pairs={{0,2},{2,4},{4,6},{6,8},{8,10},{10,12},{12,14},{14,16},{16,18},{18... | collective-permute-start | bytes 49160 | tf_op jit(solution)/shard_map/ppermute | solution.py:27
  50.5 3.2 %collective-permute-start.5 = (bf16[1,64,128]{2,1,0:T(8,128)(2,1)S(1)}, bf16[1,64,128]{2,1,0:T(8,128)(2,1)S(1)}, u32[]{:S(2)}, u32[]{:S(2)}) collective-permute-start(bf16[1,64,128]{2,1,0:T(8,128)(2,1)S(1)} %get-tuple-element.48), channel_id=1, source_target_pairs={{2,0},{4,2},{6,4},{8,6},{10,8},{12,10},{14,12},{16,14},{18,16},{20... | collective-permute-start | bytes 49160 | tf_op jit(solution)/shard_map/ppermute | solution.py:29
  54.5 1.1 collective-permute-done.5
  55.7 3.1 %collective-permute-start.6 = (bf16[6,64,1]{2,1,0:T(8,128)(2,1)S(1)}, bf16[6,64,1]{2,1,0:T(8,128)(2,1)S(1)}, u32[]{:S(2)}, u32[]{:S(2)}) collective-permute-start(bf16[6,64,1]{2,1,0:T(8,128)(2,1)S(1)} %get-tuple-element.45), channel_id=1, source_target_pairs={{0,1},{2,3},{4,5},{6,7},{8,9},{10,11},{12,13},{14,15},{16,17},{18,... | collective-permute-start | bytes 2312 | tf_op jit(solution)/shard_map/ppermute | solution.py:27
  60.5 1.3 collective-permute-start.7
  61.9 3.9 %collective-permute-done.7 = bf16[6,64,1]{2,1,0:T(8,128)(2,1)S(1)} collective-permute-done((bf16[6,64,1]{2,1,0:T(8,128)(2,1)S(1)}, bf16[6,64,1]{2,1,0:T(8,128)(2,1)S(1)}, u32[]{:S(2)}, u32[]{:S(2)}) %collective-permute-start.7) | collective-permute-done | bytes 800 | tf_op jit(solution)/shard_map/ppermute | solution.py:29
  66.6 1.5 %collective-permute-start.2 = (bf16[8,64,2]{1,2,0:T(2,128)(2,1)S(1)}, bf16[8,64,2]{1,2,0:T(2,128)(2,1)S(1)}, u32[]{:S(2)}, u32[]{:S(2)}) collective-permute-start(bf16[8,64,2]{1,2,0:T(2,128)(2,1)S(1)} %get-tuple-element.35), channel_id=1, source_target_pairs={{0,1},{2,3},{4,5},{6,7},{8,9},{10,11},{12,13},{14,15},{16,17},{18,... | collective-permute-start | bytes 6152 | tf_op jit(solution)/shard_map/ppermute | solution.py:27
  68.1 1.3 collective-permute-start.3
  70.2 2.3 %collective-permute-done.3 = bf16[8,64,2]{1,2,0:T(2,128)(2,1)S(1)} collective-permute-done((bf16[8,64,2]{1,2,0:T(2,128)(2,1)S(1)}, bf16[8,64,2]{1,2,0:T(2,128)(2,1)S(1)}, u32[]{:S(2)}, u32[]{:S(2)}) %collective-permute-start.3) | collective-permute-done | bytes 2080 | tf_op jit(solution)/shard_map/ppermute | solution.py:29
  72.6 1.0 fusion.39
  75.5 3.3 %concatenate.94 = bf16[6,576,130]{1,2,0:T(8,128)(2,1)} concatenate(bf16[6,64,130]{1,2,0:T(8,128)(2,1)S(1)} %get-tuple-element.57, bf16[6,64,130]{1,2,0:T(8,128)(2,1)} %get-tuple-element.28, bf16[6,64,130]{1,2,0:T(8,128)(2,1)S(1)} %get-tuple-element.25, bf16[6,64,130]{1,2,0:T(8,128)(2,1)S(1)} %get-tuple-element.58, bf16[6,64,130]{1,2,0:T(8,128)(2,1)} %get-tuple-element.27, ...), dimensions={1} | concatenate | bytes 1797120 | tf_op jit(solution)/shard_map/concatenate | solution.py:42
  78.7 1.9 %fusion.16 = (bf16[6,64,130]{2,1,0:T(8,128)(2,1)S(1)}, f32[6,64,130]{2,1,0:T(8,128)S(1)}) fusion(pred[6,130]{1,0:T(8,128)(4,1)S(1)} %copy-done.5, f32[64]{0:T(128)S(1)} %copy-done.6, bf16[6,576,130]{1,2,0:T(8,128)(2,1)} %concatenate.94, bf16[576,64,1]{1,0,2:T(8,128)(2,1)} %bitcast.89), kind=kOutput, calls=%fused_computation.24 | convolution fusion | flops 58056960 | bytes 1272844 | tf_op jit(solution)/shard_map/ykx,ko->yox/dot_general | solution.py:47
  80.6 1.5 %convert_reduce_fusion = (f32[64]{0:T(128)S(1)}, bf16[4,64,128]{2,1,0:T(8,128)(2,1)S(1)}) fusion(f32[6,64,130]{2,1,0:T(8,128)S(1)} %get-tuple-element.51, bf16[4,576,128]{2,1,0:T(8,128)(2,1)} %copy-done.4, bf16[576,64,1]{1,0,2:T(8,128)(2,1)} %bitcast.90), kind=kOutput, calls=%fused_computation.52 | convolution fusion | flops 38469568 | bytes 860416 | tf_op jit(solution)/shard_map/ykx,ko->yox/dot_general | solution.py:47
  82.7 1.5 %concatenate.110 = bf16[4,576,128]{1,2,0:T(8,128)(2,1)S(1)} concatenate(bf16[4,64,128]{1,2,0:T(8,128)(2,1)} %get-tuple-element.54, bf16[4,64,128]{1,2,0:T(8,128)(2,1)} %get-tuple-element.37, bf16[4,64,128]{1,2,0:T(8,128)(2,1)} %get-tuple-element.19, bf16[4,64,128]{1,2,0:T(8,128)(2,1)} %get-tuple-element.55, bf16[4,64,128]{1,2,0:T(8,128)(2,1)S(1)} %bitcast.81, ...), dimensions={1} | concatenate | bytes 1179648 | tf_op jit(solution)/shard_map/concatenate | solution.py:42
  84.2 0.9 fusion.5
  86.3 1.0 pad_maximum_fusion
  88.1 1.0 pad.9.clone
  89.1 29.0 %shard_map.165 = f32[32,24,128]{2,1,0:T(8,128)S(1)} custom-call(f32[32,24,128]{2,1,0:T(8,128)S(1)} %bitcast.76), custom_call_target="tpu_custom_call" | custom-call | tf_op jit(solution)/shard_map/pallas_call | solution.py:135
  118.1 3.4 %collective-permute-start.8 = (bf16[1,64,128]{2,1,0:T(8,128)(2,1)}, bf16[1,64,128]{2,1,0:T(8,128)(2,1)S(1)}, u32[]{:S(2)}, u32[]{:S(2)}) collective-permute-start(bf16[1,64,128]{2,1,0:T(8,128)(2,1)} %get-tuple-element.46), channel_id=1, source_target_pairs={{0,2},{2,4},{4,6},{6,8},{8,10},{10,12},{12,14},{14,16},{16,18},{18... | collective-permute-start | bytes 49160 | tf_op jit(solution)/shard_map/ppermute | solution.py:27
  121.6 1.9 %collective-permute-start.9 = (bf16[1,64,128]{2,1,0:T(8,128)(2,1)S(1)}, bf16[1,64,128]{2,1,0:T(8,128)(2,1)S(1)}, u32[]{:S(2)}, u32[]{:S(2)}) collective-permute-start(bf16[1,64,128]{2,1,0:T(8,128)(2,1)S(1)} %get-tuple-element.47), channel_id=1, source_target_pairs={{2,0},{4,2},{6,4},{8,6},{10,8},{12,10},{14,12},{16,14},{18,16},{20... | collective-permute-start | bytes 49160 | tf_op jit(solution)/shard_map/ppermute | solution.py:29
  123.5 1.3 fusion.3
  125.7 0.9 collective-permute-done.9
  126.8 3.1 %collective-permute-start.10 = (bf16[6,64,1]{2,1,0:T(8,128)(2,1)S(1)}, bf16[6,64,1]{2,1,0:T(8,128)(2,1)S(1)}, u32[]{:S(2)}, u32[]{:S(2)}) collective-permute-start(bf16[6,64,1]{2,1,0:T(8,128)(2,1)S(1)} %get-tuple-element.43), channel_id=1, source_target_pairs={{0,1},{2,3},{4,5},{6,7},{8,9},{10,11},{12,13},{14,15},{16,17},{18,... | collective-permute-start | bytes 2312 | tf_op jit(solution)/shard_map/ppermute | solution.py:27
  129.9 1.3 collective-permute-start.11
  132.4 2.8 %collective-permute-done.11 = bf16[6,64,1]{2,1,0:T(8,128)(2,1)S(1)} collective-permute-done((bf16[6,64,1]{2,1,0:T(8,128)(2,1)S(1)}, bf16[6,64,1]{2,1,0:T(8,128)(2,1)S(1)}, u32[]{:S(2)}, u32[]{:S(2)}) %collective-permute-start.11) | collective-permute-done | bytes 800 | tf_op jit(solution)/shard_map/ppermute | solution.py:29
  135.8 1.8 %fusion.7 = bf16[4,64,128]{2,1,0:T(8,128)(2,1)} fusion(bf16[4,576,128]{2,1,0:T(8,128)(2,1)S(1)} %slice_dynamic-update-slice_fusion, bf16[576,64,1]{1,0,2:T(8,128)(2,1)} %bitcast.86, bf16[4,64,128]{2,1,0:T(8,128)(2,1)S(1)} %copy-done.1), kind=kOutput, calls=%fused_computation.14 | convolution fusion | flops 37847040 | bytes 794624 | tf_op jit(solution)/shard_map/ykx,ko->yox/dot_general | solution.py:47
  (84 shorter events, 12.4 us)
Async XLA Ops:
  0.6 2.2 %copy-start = (bf16[8,64,2048]{2,1,0:T(8,128)(2,1)S(1)}, bf16[8,64,2048]{2,1,0:T(8,128)(2,1)}, u32[]{:S(2)}) copy-start(bf16[8,64,2048]{2,1,0:T(8,128)(2,1)} %param.14) | copy-start | bytes 6291460
  4.0 43.2 %copy-start.1 = (bf16[4,64,128]{2,1,0:T(8,128)(2,1)S(1)}, bf16[4,64,128]{2,1,0:T(8,128)(2,1)}, u32[]{:S(2)}) copy-start(bf16[4,64,128]{2,1,0:T(8,128)(2,1)} %param.25) | copy-start | bytes 196612
  4.0 50.4 %copy-start.2 = (bf16[9,64,64]{2,1,0:T(8,128)(2,1)S(1)}, bf16[9,64,64]{2,1,0:T(8,128)(2,1)}, u32[]{:S(2)}) copy-start(bf16[9,64,64]{2,1,0:T(8,128)(2,1)} %param.24) | copy-start | bytes 221188
  4.0 54.9 %copy-start.3 = (bf16[9,64,64]{2,1,0:T(8,128)(2,1)S(1)}, bf16[9,64,64]{2,1,0:T(8,128)(2,1)}, u32[]{:S(2)}) copy-start(bf16[9,64,64]{2,1,0:T(8,128)(2,1)} %param.22) | copy-start | bytes 221188
  42.4 24.1 %collective-permute-start = (bf16[2,64,128]{1,2,0:T(8,128)(2,1)S(1)}, bf16[2,64,128]{1,2,0:T(8,128)(2,1)S(1)}, u32[]{:S(2)}, u32[]{:S(2)}) collective-permute-start(bf16[2,64,128]{1,2,0:T(8,128)(2,1)S(1)} %bitcast.92), channel_id=1, source_target_pairs={{0,2},{2,4},{4,6},{6,8},{8,10},{10,12},{12,14},{14,16},{16,18},{18... | collective-permute-start | bytes 98312 | tf_op jit(solution)/shard_map/ppermute | solution.py:27
  44.9 21.6 %collective-permute-start.1 = (bf16[2,64,128]{1,2,0:T(8,128)(2,1)S(1)}, bf16[2,64,128]{1,2,0:T(8,128)(2,1)S(1)}, u32[]{:S(2)}, u32[]{:S(2)}) collective-permute-start(bf16[2,64,128]{1,2,0:T(8,128)(2,1)S(1)} %bitcast.93), channel_id=1, source_target_pairs={{2,0},{4,2},{6,4},{8,6},{10,8},{12,10},{14,12},{16,14},{18,16},{20... | collective-permute-start | bytes 98312 | tf_op jit(solution)/shard_map/ppermute | solution.py:29
  47.2 7.2 %collective-permute-start.4 = (bf16[1,64,128]{2,1,0:T(8,128)(2,1)S(1)}, bf16[1,64,128]{2,1,0:T(8,128)(2,1)S(1)}, u32[]{:S(2)}, u32[]{:S(2)}) collective-permute-start(bf16[1,64,128]{2,1,0:T(8,128)(2,1)S(1)} %get-tuple-element.49), channel_id=1, source_target_pairs={{0,2},{2,4},{4,6},{6,8},{8,10},{10,12},{12,14},{14,16},{16,18},{18... | collective-permute-start | bytes 49160 | tf_op jit(solution)/shard_map/ppermute | solution.py:27
  50.5 5.1 %collective-permute-start.5 = (bf16[1,64,128]{2,1,0:T(8,128)(2,1)S(1)}, bf16[1,64,128]{2,1,0:T(8,128)(2,1)S(1)}, u32[]{:S(2)}, u32[]{:S(2)}) collective-permute-start(bf16[1,64,128]{2,1,0:T(8,128)(2,1)S(1)} %get-tuple-element.48), channel_id=1, source_target_pairs={{2,0},{4,2},{6,4},{8,6},{10,8},{12,10},{14,12},{16,14},{18,16},{20... | collective-permute-start | bytes 49160 | tf_op jit(solution)/shard_map/ppermute | solution.py:29
  55.7 6.1 %collective-permute-start.6 = (bf16[6,64,1]{2,1,0:T(8,128)(2,1)S(1)}, bf16[6,64,1]{2,1,0:T(8,128)(2,1)S(1)}, u32[]{:S(2)}, u32[]{:S(2)}) collective-permute-start(bf16[6,64,1]{2,1,0:T(8,128)(2,1)S(1)} %get-tuple-element.45), channel_id=1, source_target_pairs={{0,1},{2,3},{4,5},{6,7},{8,9},{10,11},{12,13},{14,15},{16,17},{18,... | collective-permute-start | bytes 2312 | tf_op jit(solution)/shard_map/ppermute | solution.py:27
  60.5 5.3 %collective-permute-start.7 = (bf16[6,64,1]{2,1,0:T(8,128)(2,1)S(1)}, bf16[6,64,1]{2,1,0:T(8,128)(2,1)S(1)}, u32[]{:S(2)}, u32[]{:S(2)}) collective-permute-start(bf16[6,64,1]{2,1,0:T(8,128)(2,1)S(1)} %get-tuple-element.44), channel_id=1, source_target_pairs={{1,0},{3,2},{5,4},{7,6},{9,8},{11,10},{13,12},{15,14},{17,16},{19,... | collective-permute-start | bytes 2312 | tf_op jit(solution)/shard_map/ppermute | solution.py:29
  66.5 3.7 %copy-start.4 = (bf16[4,576,128]{2,1,0:T(8,128)(2,1)}, bf16[4,576,128]{2,1,0:T(8,128)(2,1)S(1)}, u32[]{:S(2)}) copy-start(bf16[4,576,128]{2,1,0:T(8,128)(2,1)S(1)} %fusion.34) | copy-start | bytes 1769476
  66.6 3.6 %collective-permute-start.2 = (bf16[8,64,2]{1,2,0:T(2,128)(2,1)S(1)}, bf16[8,64,2]{1,2,0:T(2,128)(2,1)S(1)}, u32[]{:S(2)}, u32[]{:S(2)}) collective-permute-start(bf16[8,64,2]{1,2,0:T(2,128)(2,1)S(1)} %get-tuple-element.35), channel_id=1, source_target_pairs={{0,1},{2,3},{4,5},{6,7},{8,9},{10,11},{12,13},{14,15},{16,17},{18,... | collective-permute-start | bytes 6152 | tf_op jit(solution)/shard_map/ppermute | solution.py:27
  68.1 4.4 %collective-permute-start.3 = (bf16[8,64,2]{1,2,0:T(2,128)(2,1)S(1)}, bf16[8,64,2]{1,2,0:T(2,128)(2,1)S(1)}, u32[]{:S(2)}, u32[]{:S(2)}) collective-permute-start(bf16[8,64,2]{1,2,0:T(2,128)(2,1)S(1)} %get-tuple-element.34), channel_id=1, source_target_pairs={{1,0},{3,2},{5,4},{7,6},{9,8},{11,10},{13,12},{15,14},{17,16},{19,... | collective-permute-start | bytes 6152 | tf_op jit(solution)/shard_map/ppermute | solution.py:29
  72.6 6.1 %copy-start.5 = (pred[6,130]{1,0:T(8,128)(4,1)S(1)}, pred[6,130]{1,0:T(8,128)(4,1)}, u32[]{:S(2)}) copy-start(pred[6,130]{1,0:T(8,128)(4,1)} %broadcast_and_fusion) | copy-start | bytes 2344
  72.6 6.1 %copy-start.6 = (f32[64]{0:T(128)S(1)}, f32[64]{0:T(128)}, u32[]{:S(2)}) copy-start(f32[64]{0:T(128)} %param.23) | copy-start | bytes 772
  118.1 7.6 %collective-permute-start.8 = (bf16[1,64,128]{2,1,0:T(8,128)(2,1)}, bf16[1,64,128]{2,1,0:T(8,128)(2,1)S(1)}, u32[]{:S(2)}, u32[]{:S(2)}) collective-permute-start(bf16[1,64,128]{2,1,0:T(8,128)(2,1)} %get-tuple-element.46), channel_id=1, source_target_pairs={{0,2},{2,4},{4,6},{6,8},{8,10},{10,12},{12,14},{14,16},{16,18},{18... | collective-permute-start | bytes 49160 | tf_op jit(solution)/shard_map/ppermute | solution.py:27
  121.6 5.1 %collective-permute-start.9 = (bf16[1,64,128]{2,1,0:T(8,128)(2,1)S(1)}, bf16[1,64,128]{2,1,0:T(8,128)(2,1)S(1)}, u32[]{:S(2)}, u32[]{:S(2)}) collective-permute-start(bf16[1,64,128]{2,1,0:T(8,128)(2,1)S(1)} %get-tuple-element.47), channel_id=1, source_target_pairs={{2,0},{4,2},{6,4},{8,6},{10,8},{12,10},{14,12},{16,14},{18,16},{20... | collective-permute-start | bytes 49160 | tf_op jit(solution)/shard_map/ppermute | solution.py:29
  126.8 5.6 %collective-permute-start.10 = (bf16[6,64,1]{2,1,0:T(8,128)(2,1)S(1)}, bf16[6,64,1]{2,1,0:T(8,128)(2,1)S(1)}, u32[]{:S(2)}, u32[]{:S(2)}) collective-permute-start(bf16[6,64,1]{2,1,0:T(8,128)(2,1)S(1)} %get-tuple-element.43), channel_id=1, source_target_pairs={{0,1},{2,3},{4,5},{6,7},{8,9},{10,11},{12,13},{14,15},{16,17},{18,... | collective-permute-start | bytes 2312 | tf_op jit(solution)/shard_map/ppermute | solution.py:27
  129.9 5.4 %collective-permute-start.11 = (bf16[6,64,1]{2,1,0:T(8,128)(2,1)S(1)}, bf16[6,64,1]{2,1,0:T(8,128)(2,1)S(1)}, u32[]{:S(2)}, u32[]{:S(2)}) collective-permute-start(bf16[6,64,1]{2,1,0:T(8,128)(2,1)S(1)} %get-tuple-element.42), channel_id=1, source_target_pairs={{1,0},{3,2},{5,4},{7,6},{9,8},{11,10},{13,12},{15,14},{17,16},{19,... | collective-permute-start | bytes 2312 | tf_op jit(solution)/shard_map/ppermute | solution.py:29

commit v3 on v2

--- a/solution.py
+++ b/solution.py
@@ -14,23 +14,6 @@
 HD = 128
 C = 64
 R = 4
-
-
-def with_halo(cells, sides, width):
-    for axis, dim in sides:
-        count = lax.axis_size(axis)
-        ends = count - 1
-        head = lax.slice_in_dim(cells, 0, width, axis=dim)
-        tail = lax.slice_in_dim(cells, cells.shape[dim] - width, cells.shape[dim], axis=dim)
-        cells = jnp.concatenate(
-            [
-                lax.ppermute(tail, axis, [(i, (i + 1) % count) for i in range(ends)]),
-                cells,
-                lax.ppermute(head, axis, [((i + 1) % count, i) for i in range(ends)]),
-            ],
-            axis=dim,
-        )
-    return cells
 
 
 def tap_stack(padded, height, width):
@@ -62,11 +45,72 @@
     return summed.reshape(9, padded.shape[1], grads.shape[1])
 
 
-def gradient_rim(field):
-    return with_halo(field, (("band", 0), ("var", 2)), 1)
-
-
-def sum_kernel(count, var_count, x_ref, o_ref, landed, send1, recv1, send2, recv2):
+SIDES = [(down, right) for down in (-1, 0, 1) for right in (-1, 0, 1) if down or right]
+
+
+def present(bands, parts, down, right):
+    band = lax.axis_index("band") + down
+    var = lax.axis_index("var") + right
+    return (band >= 0) & (band < bands) & (var >= 0) & (var < parts)
+
+
+def to_sides(bands, parts, pieces, out_sem, in_sem):
+    copies = []
+    for index, (down, right) in enumerate(SIDES):
+        source, target = pieces(down, right)
+        copies.append(
+            pltpu.make_async_remote_copy(
+                src_ref=source,
+                dst_ref=target,
+                send_sem=out_sem.at[index],
+                recv_sem=in_sem.at[index],
+                device_id=(lax.axis_index("band") + down, lax.axis_index("var") + right),
+                device_id_type=MESH,
+            )
+        )
+
+    def start():
+        for copy, (down, right) in zip(copies, SIDES):
+            pl.when(present(bands, parts, down, right))(copy.start)
+
+    def take():
+        for copy, (down, right) in zip(copies, SIDES):
+            pl.when(present(bands, parts, -down, -right))(copy.wait_recv)
+
+    def finish():
+        for copy, (down, right) in zip(copies, SIDES):
+            pl.when(present(bands, parts, down, right))(copy.wait_send)
+
+    return start, take, finish
+
+
+def rim_pieces(field, rim):
+    height = field.shape[0]
+
+    def pieces(down, right):
+        take, put = {-1: (0, height + 1), 0: (0, 1), 1: (height - 1, 0)}[down]
+        size = 1 if down else height
+        return field.at[pl.ds(take, size)], rim.at[1 - right, pl.ds(put, size)]
+
+    return pieces
+
+
+def rim_shape(field):
+    return jax.ShapeDtypeStruct((3, field.shape[0] + 2) + field.shape[1:], field.dtype)
+
+
+def padded_from(rim):
+    return jnp.concatenate([rim[0, :, :, -1:], rim[1], rim[2, :, :, :1]], axis=2)
+
+
+def sum_kernel(
+    count, var_count, x_ref, field_ref, o_ref, rim_ref,
+    landed, send1, recv1, send2, recv2, rim_out, rim_in,
+):
+    rim_ref[...] = jnp.zeros_like(rim_ref)
+    rim_start, rim_take, rim_finish = to_sides(
+        count // var_count, var_count, rim_pieces(field_ref, rim_ref), rim_out, rim_in
+    )
     me = lax.axis_index("band") * var_count + lax.axis_index("var")
 
     def place(device):
@@ -102,6 +146,8 @@
         )
 
     pl.semaphore_wait(barrier, count - 1)
+    rim_start()
+    rim_ref[1, 1 : field_ref.shape[0] + 1] = field_ref[...]
 
     @pl.loop(1, count)
     def _(step):
@@ -126,35 +172,45 @@
         scatter(step).wait_send()
         spread(step, me).wait_send()
 
-
-def sum_everywhere(terms, band_count, var_count):
+    rim_take()
+    rim_finish()
+
+
+def sum_everywhere(terms, field, band_count, var_count):
     count = band_count * var_count
     rows = -(-terms.shape[0] // (8 * count)) * 8
     padded = jnp.pad(terms, ((0, rows * count - terms.shape[0]), (0, 0)))
     slots = (count, rows, terms.shape[1])
-    summed = pl.pallas_call(
+    vmem = pl.BlockSpec(memory_space=pltpu.VMEM)
+    summed, rim = pl.pallas_call(
         functools.partial(sum_kernel, count, var_count),
-        out_shape=jax.ShapeDtypeStruct(slots, jnp.float32),
-        in_specs=[pl.BlockSpec(memory_space=pltpu.VMEM)],
-        out_specs=pl.BlockSpec(memory_space=pltpu.VMEM),
+        out_shape=(jax.ShapeDtypeStruct(slots, jnp.float32), rim_shape(field)),
+        in_specs=[vmem, vmem],
+        out_specs=(vmem, vmem),
         scratch_shapes=[pltpu.VMEM(slots, jnp.float32)]
-        + [pltpu.SemaphoreType.DMA((count,)) for _ in range(4)],
+        + [pltpu.SemaphoreType.DMA((count,)) for _ in range(4)]
+        + [pltpu.SemaphoreType.DMA((8,)) for _ in range(2)],
         compiler_params=pltpu.CompilerParams(
             collective_id=0, has_side_effects=True, vmem_limit_bytes=32 << 20
         ),
-    )(padded.reshape(slots))
-    return summed.reshape(rows * count, terms.shape[1])
+    )(padded.reshape(slots), field)
+    return summed.reshape(rows * count, terms.shape[1]), padded_from(rim)
 
 
 def token_kernel(
     bands, heads, parts,
-    mix_ref, gain_ref, wq_any, wk_any, wv_any, wo_any, up_any,
-    o_ref,
+    mix_ref, gain_ref, field_ref, wq_any, wk_any, wv_any, wo_any, up_any,
+    o_ref, rim_ref,
     wq, wk, wv, wo, up, mixes, normed, query, key, value, query_all, key_all, value_all,
     context, joined, partial, slabs,
     load, mix_out, mix_in, key_out, key_in, value_out, value_in, query_out, query_in,
-    context_out, context_in, slab_out, slab_in,
+    context_out, context_in, slab_out, slab_in, rim_out, rim_in, fine_out, fine_in,
 ):
+    o_ref[...] = jnp.zeros_like(o_ref)
+    rim_ref[...] = jnp.zeros_like(rim_ref)
+    rim_start, rim_take, rim_finish = to_sides(
+        bands, parts, rim_pieces(field_ref, rim_ref), rim_out, rim_in
+    )
     band = lax.axis_index("band")
     var = lax.axis_index("var")
     rows = mix_ref.shape[0]
@@ -226,7 +282,34 @@
             slab_out.at[step], slab_in.at[step], band, peer,
         )
 
+    middle = up_any.shape[1] // 2
+
+    def fine_pieces(down, right):
+        take, put = {-1: (1, 3), 0: (1, 1), 1: (2, 0)}[down]
+        size = middle if down else 2 * middle
+        start, land, length = {
+            -1: (16, 16 + slab_rows, 16),
+            0: (16, 16, slab_rows),
+            1: (slab_rows, 0, 16),
+        }[right]
+        return (
+            o_ref.at[pl.ds(start, length), pl.ds(take * middle, size)],
+            o_ref.at[pl.ds(land, length), pl.ds(put * middle, size)],
+        )
+
+    fine_start, fine_take, fine_finish = to_sides(bands, parts, fine_pieces, fine_out, fine_in)
     barrier = pltpu.get_barrier_semaphore()
+    corners = 0
+    for down, right in SIDES:
+        if down and right:
+            there = present(bands, parts, down, right)
+            corners = corners + there.astype(jnp.int32)
+
+            @pl.when(there)
+            def _():
+                pl.semaphore_signal(
+                    barrier, inc=1, device_id=(band + down, var + right), device_id_type=MESH
+                )
 
     @pl.loop(1, parts)
     def _(step):
@@ -248,9 +331,11 @@
     ]
     for item in loads:
         item.start()
-    pl.semaphore_wait(barrier, bands + parts - 2)
+    pl.semaphore_wait(barrier, bands + parts - 2 + corners)
     for step in range(1, parts):
         send_mix(step).start()
+    rim_start()
+    rim_ref[1, 1 : field_ref.shape[0] + 1] = field_ref[...]
     mixed = mix_ref[...].astype(jnp.float32)
     for step in range(1, parts):
         send_mix(step).wait_recv()
@@ -357,7 +442,12 @@
         send_slab(step).wait_recv()
         hidden = hidden + slabs[step].astype(jnp.float32)
     hidden = (hidden + normed[lines(var, slab_rows), :].astype(jnp.float32)).astype(jnp.bfloat16)
-    o_ref[...] = jnp.dot(hidden, up[...], preferred_element_type=jnp.float32).astype(jnp.bfloat16)
+    o_ref[16 : 16 + slab_rows, middle : 3 * middle] = jnp.dot(
+        hidden, up[...], preferred_element_type=jnp.float32
+    ).astype(jnp.bfloat16)
+    fine_start()
+    rim_take()
+    rim_finish()
 
     for step in range(1, parts):
         send_mix(step).wait_send()
@@ -373,8 +463,11 @@
         send_query(step).wait_send()
         send_context(other_head(step)).wait_send()
 
-
-def token_stage(own_mix, agg_gain, wq, wk, wv, wo, w_up, bands, parts):
+    fine_take()
+    fine_finish()
+
+
+def token_stage(own_mix, agg_gain, field, wq, wk, wv, wo, w_up, bands, parts):
     rows = own_mix.shape[0]
     wide = wq.shape[1]
     heads = wide // HD
@@ -389,9 +482,12 @@
     vmem = pl.BlockSpec(memory_space=pltpu.VMEM)
     return pl.pallas_call(
         functools.partial(token_kernel, bands, heads, parts),
-        out_shape=jax.ShapeDtypeStruct((rows // parts, fine), jnp.bfloat16),
-        in_specs=[vmem, vmem] + [pl.BlockSpec(memory_space=pl.ANY)] * 5,
-        out_specs=vmem,
+        out_shape=(
+            jax.ShapeDtypeStruct((rows // parts + 32, 2 * fine), jnp.bfloat16),
+            rim_shape(field),
+        ),
+        in_specs=[vmem] * 3 + [pl.BlockSpec(memory_space=pl.ANY)] * 5,
+        out_specs=(vmem, vmem),
         scratch_shapes=[
             half(D, wide), half(D, wide), half(D, wide), half(wide, D), half(D, fine),
             half(parts, rows, D), half(rows, D),
@@ -401,12 +497,12 @@
             half(parts, rows // parts, D),
             flags(5), flags(parts), flags(parts), flags(bands), flags(bands), flags(bands),
             flags(bands), flags(heads), flags(heads), flags(heads), flags(heads),
-            flags(parts), flags(parts),
+            flags(parts), flags(parts), flags(8), flags(8), flags(8), flags(8),
         ],
         compiler_params=pltpu.CompilerParams(
             collective_id=1, has_side_effects=True, vmem_limit_bytes=56 << 20
         ),
-    )(own_mix, agg_gain[None], wq, wk, wv, wo, w_up)
+    )(own_mix, agg_gain[None], field, wq, wk, wv, wo, w_up)
 
 
 def on_device(
@@ -426,16 +522,17 @@
     token_rows = jnp.transpose(
         own_mix.reshape(lat_dev, var_count, lon_dev, D), (1, 0, 2, 3)
     ).reshape(-1, D)
-    upsampled = token_stage(
-        token_rows, agg_gain, wq, wk, wv, wo, w_up, band_count, var_count
+    around, rim = token_stage(
+        token_rows, agg_gain, cotangent, wq, wk, wv, wo, w_up, band_count, var_count
     )
     height = lat_dev * R
     width = lon_dev * R
-    upsampled = jnp.transpose(
-        upsampled.reshape(lat_dev, lon_dev, R, R, C), (0, 2, 4, 1, 3)
-    ).reshape(height, C, width)
+    fine_wide = jnp.transpose(
+        around.reshape(lon_dev + 32, 2 * R, R, C), (1, 3, 0, 2)
+    ).reshape(2 * R, C, width + 32 * R)
+    widened = fine_wide[:, :, 16 * R - 2 : 16 * R + width + 2]
+    upsampled = fine_wide[2 : 2 + height, :, 16 * R : 16 * R + width]
     bias_cols = bias1[None, :, None]
-    widened = with_halo(upsampled, (("band", 0), ("var", 2)), 2)
     pre_wide = conv_padded(widened, conv1, height + 2, width + 2) + bias_cols
     row_ids = lax.axis_index("band") * height + jnp.arange(height + 2) - 1
     col_ids = lax.axis_index("var") * width + jnp.arange(width + 2) - 1
@@ -448,20 +545,21 @@
     field_out = (
         conv_padded(active_pad, conv2, height, width) + upsampled.astype(jnp.float32)
     ).astype(jnp.bfloat16)
-    cotangent_pad = gradient_rim(cotangent)
+    cotangent_pad = padded_from(rim)
     d_active = conv_padded(cotangent_pad, flipped(conv2), height, width)
     d_pre = jax.vjp(jax.nn.gelu, pre)[1](d_active)[0].astype(jnp.bfloat16)
-    d_pre_pad = gradient_rim(d_pre)
-    grad_fine = (
-        cotangent.astype(jnp.float32) + conv_padded(d_pre_pad, flipped(conv1), height, width)
-    ).astype(jnp.bfloat16)
     factor = 1.0 / math.sqrt(height * band_count * width * var_count)
     first_terms = weight_grad(fine_pad, d_pre).reshape(9 * C, C) * factor
     second_terms = weight_grad(active_pad, cotangent).reshape(9 * C, C) * factor
     bias_terms = jnp.sum(d_pre.astype(jnp.float32), axis=(0, 2)) * factor
     terms = jnp.concatenate([first_terms, second_terms], axis=1)
     bias_row = jnp.pad(bias_terms, (0, C))[None]
-    summed = sum_everywhere(jnp.concatenate([terms, bias_row], axis=0), band_count, var_count)
+    summed, d_pre_pad = sum_everywhere(
+        jnp.concatenate([terms, bias_row], axis=0), d_pre, band_count, var_count
+    )
+    grad_fine = (
+        cotangent.astype(jnp.float32) + conv_padded(d_pre_pad, flipped(conv1), height, width)
+    ).astype(jnp.bfloat16)
     grad_conv1 = summed[: 9 * C, :C].reshape(9, C, C)
     grad_conv2 = summed[: 9 * C, C:].reshape(9, C, C)
     grad_bias = summed[9 * C, :C]

time: 140 us -> 99.6 us (0.71); the launches traced: 138 us -> 98.9 us
  starting transfers between devices: 28.2 us -> 0 us
  waiting for transfers between devices: 11.1 us -> 0 us
  other arithmetic: 4.4 us -> 2.38 us
  Pallas kernels: 66.3 us -> 68.1 us
    ppermute x12 -> x0, starting transfers between devices: 28.2 us -> none  [the longest x6 17 us: with_halo(): lax.ppermute(tail, axis, [(i, (i + 1) % count) for i in range(ends)])]
    ppermute x12 -> x0, waiting for transfers between devices: 11.1 us -> none  [the longest x6 11.1 us: with_halo(): lax.ppermute(head, axis, [((i + 1) % count, i) for i in range(ends)])]
    pallas_call x1, Pallas kernels: 37.3 us -> 42.3 us  [token_stage(): pl.pallas_call(functools.partial(token_kernel, bands, heads, parts), out_...]
    pallas_call x1, Pallas kernels: 29 us -> 25.9 us  [sum_everywhere(): pl.pallas_call(functools.partial(sum_kernel, count, var_count), out_shape...]
    unnamed x33 -> x28, local copies, waits for them, and re-layouts: 2.5 us -> 3.52 us
    concatenate x4 -> x3, local copies, waits for them, and re-layouts: 4.94 us -> 4.93 us  [tap_stack(): return jnp.concatenate(pieces, axis=1)]
  transfers between devices with their start and end apart: 12 -> 0, of which waited for: 5 -> 0; matrix products, arithmetic and copies ran while one was open for 5% -> 0% of each run, Pallas kernels for 0% -> 0%
where the time goes in v3:
time: 99.6 us; the launch traced here: 98.9 us
  Pallas kernels  68.1 us (68%)
  local copies, waits for them, and re-layouts  17.9 us (18%)
  matrix products  9.6 us (10%)
  other arithmetic  2.38 us (2%)
    pallas_call x1, Pallas kernels, token_stage(): pl.pallas_call(functools.partial(token_kernel, bands, heads, parts), out_...  42.3 us
    pallas_call x1, Pallas kernels, sum_everywhere(): pl.pallas_call(functools.partial(sum_kernel, count, var_count), out_shape...  25.9 us
    dot_general x4, matrix products, conv_padded(): jnp.einsum('ykx,ko->yox', stacked, weight.reshape(-1, weight.shape[2]), p...  7.04 us
    concatenate x3, local copies, waits for them, and re-layouts, tap_stack(): return jnp.concatenate(pieces, axis=1)  4.93 us
    unnamed x28, local copies, waits for them, and re-layouts  3.52 us
    transpose x4, local copies, waits for them, and re-layouts, flipped(): return jnp.transpose(weight[::-1], (0, 2, 1))  2.14 us
    slice x2, local copies, waits for them, and re-layouts, tap_stack(): padded[row_tap:row_tap + height, :, col_tap:col_tap + width]  2 us

profile of v3, /device:TPU:25, one launch (start us, length us, event | category | flops | bytes accessed | tf_op | source)
XLA Modules:
  0.0 98.9 jit_solution(8281021482411010577)
XLA Ops:
  0.8 1.1 %copy.30 = bf16[1,64,8,64]{3,2,1,0:T(8,128)(2,1)S(1)} copy(bf16[1,64,8,64]{3,1,0,2:T(8,128)(2,1)} %bitcast.109) | data formatting | bytes 131072 | tf_op jit(solution)/shard_map/transpose | solution.py:515
  1.9 0.1 reshape.100
  2.0 0.3 copy-done
  2.3 0.9 reduce_sum.18
  3.2 1.2 %fusion.mix_ref = bf16[64,2048]{1,0:T(8,128)(2,1)} fusion(bf16[64,512]{1,0:T(8,128)(2,1)S(1)} %reshape.100, bf16[512,2048]{1,0:T(8,128)(2,1)S(1)} %bitcast.95, f32[2048]{0:T(1024)S(1)} %reduce_sum.18), kind=kOutput, calls=%fused_computation.1 | convolution fusion | flops 134479872 | bytes 2433024 | tf_op jit(solution)/shard_map/dot_general | solution.py:518
  4.3 42.3 %shard_map.164 = (bf16[64,2048]{1,0:T(8,128)(2,1)}, bf16[3,6,64,128]{3,2,1,0:T(8,128)(2,1)}) custom-call(bf16[64,2048]{1,0:T(8,128)(2,1)} %fusion.mix_ref, f32[1,2048]{1,0:T(1,128)} %bitcast.110, bf16[4,64,128]{2,1,0:T(8,128)(2,1)} %field_ref.1, bf16[2048,1024]{1,0:T(8,128)(2,1)} %wq_any.1, bf16[2048,1024]{1,0:T(8,128)(2,1)} %wk_any.1, ...), custom_call_target="tpu_custom_call" | custom-call | tf_op jit(solution)/shard_map/pallas_call | solution.py:483
  46.6 1.5 %reshape.102 = bf16[64,8,4,64]{3,2,1,0:T(4,128)(2,1)S(1)} reshape(bf16[64,2048]{1,0:T(8,128)(2,1)} %get-tuple-element.9) | data formatting | bytes 524288 | tf_op jit(solution)/shard_map/reshape | solution.py:531
  48.1 0.2 copy.31
  48.3 1.0 %fusion.45 = (bf16[6,64,130]{1,2,0:T(8,128)(2,1)S(1)}, bf16[6,64,130]{1,2,0:T(8,128)(2,1)S(1)}, bf16[6,64,130]{1,2,0:T(8,128)(2,1)S(1)}, bf16[6,64,130]{1,2,0:T(...) fusion(bf16[8,64,256]{1,2,0:T(8,128)(2,1)S(1)} %bitcast.99), kind=kLoop, calls=%fused_computation.106 | loop fusion | bytes 1797120 | tf_op jit(solution)/shard_map/slice | solution.py:21
  49.3 3.4 %concatenate.44 = bf16[6,576,130]{1,2,0:T(8,128)(2,1)} concatenate(bf16[6,64,130]{1,2,0:T(8,128)(2,1)} %get-tuple-element.40, bf16[6,64,130]{1,2,0:T(8,128)(2,1)} %get-tuple-element.39, bf16[6,64,130]{1,2,0:T(8,128)(2,1)} %get-tuple-element.38, bf16[6,64,130]{1,2,0:T(8,128)(2,1)} %get-tuple-element.37, bf16[6,64,130]{1,2,0:T(8,128)(2,1)} %get-tuple-element.36, ...), dimensions={1} | concatenate | bytes 1797120 | tf_op jit(solution)/shard_map/concatenate | solution.py:25
  52.7 2.6 %fusion.16 = (bf16[6,64,130]{2,1,0:T(8,128)(2,1)S(1)}, f32[6,64,130]{2,1,0:T(8,128)}) fusion(pred[6,130]{1,0:T(8,128)(4,1)S(1)} %broadcast_and_fusion, f32[64]{0:T(128)S(1)} %copy-done.5, bf16[6,576,130]{1,2,0:T(8,128)(2,1)} %concatenate.44, bf16[576,64,1]{1,0,2:T(8,128)(2,1)} %bitcast.107), kind=kOutput, calls=%fused_computation.24 | convolution fusion | flops 58056960 | bytes 1272844 | tf_op jit(solution)/shard_map/ykx,ko->yox/dot_general | solution.py:30
  56.1 1.9 %fusion.3 = bf16[4,64,128]{1,2,0:T(8,128)(2,1)} fusion(bf16[4,576,128]{2,1,0:T(8,128)(2,1)S(1)} %slice_dynamic-update-slice_fusion, bf16[576,64,1]{1,0,2:T(8,128)(2,1)} %bitcast.103, bf16[8,64,256]{1,2,0:T(8,128)(2,1)S(1)} %bitcast.100), kind=kOutput, calls=%fused_computation.6 | convolution fusion | flops 37847040 | bytes 794624 | tf_op jit(solution)/shard_map/ykx,ko->yox/dot_general | solution.py:30
  58.0 1.6 %copy.46 = bf16[4,64,128]{2,1,0:T(8,128)(2,1)} copy(bf16[4,64,128]{1,2,0:T(8,128)(2,1)} %fusion.3) | data formatting | bytes 131072
  59.9 0.1 fusion.35
  60.1 0.1 fusion.33
  60.4 0.1 fusion.42
  60.5 0.8 copy-done.4
  61.3 0.9 reverse_bitcast_fusion.1
  62.3 0.1 copy.37
  62.4 1.5 %convert_reduce_fusion = (f32[64]{0:T(128)S(1)}, bf16[4,64,128]{2,1,0:T(8,128)(2,1)S(1)}) fusion(f32[6,64,130]{2,1,0:T(8,128)} %get-tuple-element.48, bf16[4,576,128]{2,1,0:T(8,128)(2,1)} %copy-done.4, bf16[576,64,1]{1,0,2:T(8,128)(2,1)S(1)} %bitcast.108), kind=kOutput, calls=%fused_computation.53 | convolution fusion | flops 38469568 | bytes 860416 | tf_op jit(solution)/shard_map/ykx,ko->yox/dot_general | solution.py:30
  64.0 0.7 copy.40
  64.7 1.1 %fusion.4 = f32[576,64]{0,1:T(8,128)S(1)} fusion(bf16[4,576,128]{2,1,0:T(8,128)(2,1)S(1)} %slice_dynamic-update-slice_fusion, bf16[4,64,128]{2,1,0:T(8,128)(2,1)} %field_ref.1), kind=kOutput, calls=%fused_computation.9 | convolution fusion | flops 37785600 | bytes 802816 | tf_op jit(solution)/shard_map/ykx,yox->ko/dot_general | solution.py:44
  65.9 0.9 fusion.44
  66.8 1.4 %concatenate.46 = bf16[4,576,128]{1,2,0:T(8,128)(2,1)S(1)} concatenate(bf16[4,64,128]{1,2,0:T(8,128)(2,1)} %get-tuple-element.30, bf16[4,64,128]{1,2,0:T(8,128)(2,1)} %get-tuple-element.29, bf16[4,64,128]{1,2,0:T(8,128)(2,1)} %get-tuple-element.28, bf16[4,64,128]{1,2,0:T(8,128)(2,1)} %get-tuple-element.27, bf16[4,64,128]{1,2,0:T(8,128)(2,1)} %get-tuple-element.31, ...), dimensions={1} | concatenate | bytes 1179648 | tf_op jit(solution)/shard_map/concatenate | solution.py:25
  68.3 0.2 fusion.5
  68.6 0.1 copy.57
  68.8 25.9 %shard_map.165 = (f32[32,24,128]{2,1,0:T(8,128)S(1)}, bf16[3,6,64,128]{3,2,1,0:T(8,128)(2,1)S(1)}) custom-call(f32[32,24,128]{2,1,0:T(8,128)S(1)} %bitcast.96, bf16[4,64,128]{2,1,0:T(8,128)(2,1)S(1)} %get-tuple-element.50.field_ref), custom_call_target="tpu_custom_call" | custom-call | tf_op jit(solution)/shard_map/pallas_call | solution.py:185
  95.6 0.9 reverse_bitcast_fusion
  96.5 0.1 copy.44
  96.6 0.9 fusion.7
  97.5 0.9 fusion.46
  98.4 0.5 slice_bitcast_fusion.6
  (45 shorter events, 2.2 us)
Async XLA Ops:
  0.6 1.7 %copy-start = (bf16[8,64,2048]{2,1,0:T(8,128)(2,1)S(1)}, bf16[8,64,2048]{2,1,0:T(8,128)(2,1)}, u32[]{:S(2)}) copy-start(bf16[8,64,2048]{2,1,0:T(8,128)(2,1)} %param.14) | copy-start | bytes 6291460
  46.6 6.1 %copy-start.5 = (f32[64]{0:T(128)S(1)}, f32[64]{0:T(128)}, u32[]{:S(2)}) copy-start(f32[64]{0:T(128)} %param.23) | copy-start | bytes 772
  52.7 6.9 %copy-start.1 = (bf16[3,6,64,128]{3,2,1,0:T(8,128)(2,1)S(1)}, bf16[3,6,64,128]{3,2,1,0:T(8,128)(2,1)}, u32[]{:S(2)}) copy-start(bf16[3,6,64,128]{3,2,1,0:T(8,128)(2,1)} %get-tuple-element.10) | copy-start | bytes 884740
  60.5 0.8 copy-start.4
  65.9 2.7 %copy-start.3 = (f32[1,128]{0,1:T(8,128)S(1)}, f32[1,128]{0,1:T(8,128)}, u32[]{:S(2)}) copy-start(f32[1,128]{0,1:T(8,128)} %copy.40) | copy-start | bytes 1540
  66.8 29.8 %copy-start.2 = (bf16[4,64,128]{2,1,0:T(8,128)(2,1)S(1)}, bf16[4,64,128]{2,1,0:T(8,128)(2,1)}, u32[]{:S(2)}) copy-start(bf16[4,64,128]{2,1,0:T(8,128)(2,1)} %field_ref.1) | copy-start | bytes 196612

commit v4 on v3

--- a/solution.py
+++ b/solution.py
@@ -105,7 +105,7 @@
 
 def sum_kernel(
     count, var_count, x_ref, field_ref, o_ref, rim_ref,
-    landed, send1, recv1, send2, recv2, rim_out, rim_in,
+    paired, sums, landed, pair_out, pair_in, send1, recv1, send2, recv2, rim_out, rim_in,
 ):
     rim_ref[...] = jnp.zeros_like(rim_ref)
     rim_start, rim_take, rim_finish = to_sides(
@@ -116,26 +116,45 @@
     def place(device):
         return (lax.div(device, var_count), lax.rem(device, var_count))
 
+    half = count // 2
+    band = lax.axis_index("band")
+    core = lax.rem(band, 2)
+    group = lax.div(band, 2) * var_count + lax.axis_index("var")
+    mine = core * half
+
+    def in_group(index):
+        return (lax.div(index, var_count) * 2 + core, lax.rem(index, var_count))
+
+    def remote(source, target, out_sem, in_sem, device):
+        return pltpu.make_async_remote_copy(
+            src_ref=source,
+            dst_ref=target,
+            send_sem=out_sem,
+            recv_sem=in_sem,
+            device_id=device,
+            device_id_type=MESH,
+        )
+
+    partner = (band + 1 - 2 * core, lax.axis_index("var"))
+
+    def give_half():
+        theirs = pl.ds((1 - core) * half, half)
+        return remote(x_ref.at[theirs], paired, pair_out.at[0], pair_in.at[0], partner)
+
+    def share_half(owner):
+        part = pl.ds(owner * half, half)
+        return remote(o_ref.at[part], o_ref.at[part], pair_out.at[1], pair_in.at[1], partner)
+
     def scatter(step):
-        peer = lax.rem(me + step, count)
-        return pltpu.make_async_remote_copy(
-            src_ref=x_ref.at[peer],
-            dst_ref=landed.at[step],
-            send_sem=send1.at[step],
-            recv_sem=recv1.at[step],
-            device_id=place(peer),
-            device_id_type=MESH,
+        peer = lax.rem(group + step, half)
+        return remote(
+            sums.at[peer], landed.at[step], send1.at[step], recv1.at[step], in_group(peer)
         )
 
     def spread(step, owner):
-        return pltpu.make_async_remote_copy(
-            src_ref=o_ref.at[owner],
-            dst_ref=o_ref.at[owner],
-            send_sem=send2.at[step],
-            recv_sem=recv2.at[step],
-            device_id=place(lax.rem(me + step, count)),
-            device_id_type=MESH,
-        )
+        peer = lax.rem(group + step, half)
+        slot = o_ref.at[mine + owner]
+        return remote(slot, slot, send2.at[step], recv2.at[step], in_group(peer))
 
     barrier = pltpu.get_barrier_semaphore()
 
@@ -146,10 +165,17 @@
         )
 
     pl.semaphore_wait(barrier, count - 1)
+    give_half().start()
     rim_start()
     rim_ref[1, 1 : field_ref.shape[0] + 1] = field_ref[...]
 
-    @pl.loop(1, count)
+    give_half().wait_recv()
+
+    @pl.loop(0, half)
+    def _(index):
+        sums[index] = x_ref[mine + index] + paired[index]
+
+    @pl.loop(1, half)
     def _(step):
         scatter(step).start()
 
@@ -157,21 +183,26 @@
         scatter(step).wait_recv()
         return total + landed[step]
 
-    o_ref[me] = lax.fori_loop(1, count, add, x_ref[me])
-
-    @pl.loop(1, count)
-    def _(step):
-        spread(step, me).start()
-
-    @pl.loop(1, count)
-    def _(step):
-        spread(step, lax.rem(me - step + count, count)).wait_recv()
-
-    @pl.loop(1, count)
+    o_ref[mine + group] = lax.fori_loop(1, half, add, sums[group])
+
+    @pl.loop(1, half)
+    def _(step):
+        spread(step, group).start()
+
+    @pl.loop(1, half)
+    def _(step):
+        spread(step, lax.rem(group - step + half, half)).wait_recv()
+
+    share_half(core).start()
+    give_half().wait_send()
+
+    @pl.loop(1, half)
     def _(step):
         scatter(step).wait_send()
-        spread(step, me).wait_send()
-
+        spread(step, group).wait_send()
+
+    share_half(1 - core).wait_recv()
+    share_half(core).wait_send()
     rim_take()
     rim_finish()
 
@@ -187,8 +218,9 @@
         out_shape=(jax.ShapeDtypeStruct(slots, jnp.float32), rim_shape(field)),
         in_specs=[vmem, vmem],
         out_specs=(vmem, vmem),
-        scratch_shapes=[pltpu.VMEM(slots, jnp.float32)]
-        + [pltpu.SemaphoreType.DMA((count,)) for _ in range(4)]
+        scratch_shapes=[pltpu.VMEM((count // 2,) + slots[1:], jnp.float32) for _ in range(3)]
+        + [pltpu.SemaphoreType.DMA((2,)) for _ in range(2)]
+        + [pltpu.SemaphoreType.DMA((count // 2,)) for _ in range(4)]
         + [pltpu.SemaphoreType.DMA((8,)) for _ in range(2)],
         compiler_params=pltpu.CompilerParams(
             collective_id=0, has_side_effects=True, vmem_limit_bytes=32 << 20

time: 99.6 us -> 94.3 us (0.947)
  the two profiles are of different devices: /device:TPU:25 before, /device:TPU:0 now
where the time goes in v4:
time: 94.3 us; the launch traced here: 93.6 us
  Pallas kernels  62.8 us (67%)
  local copies, waits for them, and re-layouts  17.9 us (19%)
  matrix products  9.61 us (10%)
  other arithmetic  2.38 us (3%)
  between operations  0.95 us (1%)
    pallas_call x1, Pallas kernels, token_stage(): pl.pallas_call(functools.partial(token_kernel, bands, heads, parts), out_...  44 us
    pallas_call x1, Pallas kernels, sum_everywhere(): pl.pallas_call(functools.partial(sum_kernel, count, var_count), out_shape...  18.8 us
    dot_general x4, matrix products, conv_padded(): jnp.einsum('ykx,ko->yox', stacked, weight.reshape(-1, weight.shape[2]), p...  7.05 us
    concatenate x3, local copies, waits for them, and re-layouts, tap_stack(): return jnp.concatenate(pieces, axis=1)  4.93 us
    unnamed x28, local copies, waits for them, and re-layouts  3.52 us
    transpose x4, local copies, waits for them, and re-layouts, flipped(): return jnp.transpose(weight[::-1], (0, 2, 1))  2.14 us
    slice x2, local copies, waits for them, and re-layouts, tap_stack(): padded[row_tap:row_tap + height, :, col_tap:col_tap + width]  2 us

profile of v4, /device:TPU:0, one launch (start us, length us, event | category | flops | bytes accessed | tf_op | source)
XLA Modules:
  0.0 93.6 jit_solution(12356728085729801387)
XLA Ops:
  0.8 1.1 %copy.30 = bf16[1,64,8,64]{3,2,1,0:T(8,128)(2,1)S(1)} copy(bf16[1,64,8,64]{3,1,0,2:T(8,128)(2,1)} %bitcast.109) | data formatting | bytes 131072 | tf_op jit(solution)/shard_map/transpose | solution.py:547
  1.9 0.1 reshape.100
  2.0 0.3 copy-done
  2.3 0.9 reduce_sum.18
  3.2 1.2 %fusion.mix_ref = bf16[64,2048]{1,0:T(8,128)(2,1)} fusion(bf16[64,512]{1,0:T(8,128)(2,1)S(1)} %reshape.100, bf16[512,2048]{1,0:T(8,128)(2,1)S(1)} %bitcast.95, f32[2048]{0:T(1024)S(1)} %reduce_sum.18), kind=kOutput, calls=%fused_computation.1 | convolution fusion | flops 134479872 | bytes 2433024 | tf_op jit(solution)/shard_map/dot_general | solution.py:550
  4.3 44.0 %shard_map.164 = (bf16[64,2048]{1,0:T(8,128)(2,1)}, bf16[3,6,64,128]{3,2,1,0:T(8,128)(2,1)}) custom-call(bf16[64,2048]{1,0:T(8,128)(2,1)} %fusion.mix_ref, f32[1,2048]{1,0:T(1,128)} %bitcast.110, bf16[4,64,128]{2,1,0:T(8,128)(2,1)} %field_ref.1, bf16[2048,1024]{1,0:T(8,128)(2,1)} %wq_any.1, bf16[2048,1024]{1,0:T(8,128)(2,1)} %wk_any.1, ...), custom_call_target="tpu_custom_call" | custom-call | tf_op jit(solution)/shard_map/pallas_call | solution.py:515
  48.3 1.5 %reshape.102 = bf16[64,8,4,64]{3,2,1,0:T(4,128)(2,1)S(1)} reshape(bf16[64,2048]{1,0:T(8,128)(2,1)} %get-tuple-element.9) | data formatting | bytes 524288 | tf_op jit(solution)/shard_map/reshape | solution.py:563
  49.8 0.2 copy.31
  50.0 1.0 %fusion.45 = (bf16[6,64,130]{1,2,0:T(8,128)(2,1)S(1)}, bf16[6,64,130]{1,2,0:T(8,128)(2,1)S(1)}, bf16[6,64,130]{1,2,0:T(8,128)(2,1)S(1)}, bf16[6,64,130]{1,2,0:T(...) fusion(bf16[8,64,256]{1,2,0:T(8,128)(2,1)S(1)} %bitcast.99), kind=kLoop, calls=%fused_computation.106 | loop fusion | bytes 1797120 | tf_op jit(solution)/shard_map/slice | solution.py:21
  51.0 3.4 %concatenate.44 = bf16[6,576,130]{1,2,0:T(8,128)(2,1)} concatenate(bf16[6,64,130]{1,2,0:T(8,128)(2,1)} %get-tuple-element.40, bf16[6,64,130]{1,2,0:T(8,128)(2,1)} %get-tuple-element.39, bf16[6,64,130]{1,2,0:T(8,128)(2,1)} %get-tuple-element.38, bf16[6,64,130]{1,2,0:T(8,128)(2,1)} %get-tuple-element.37, bf16[6,64,130]{1,2,0:T(8,128)(2,1)} %get-tuple-element.36, ...), dimensions={1} | concatenate | bytes 1797120 | tf_op jit(solution)/shard_map/concatenate | solution.py:25
  54.5 2.7 %fusion.16 = (bf16[6,64,130]{2,1,0:T(8,128)(2,1)S(1)}, f32[6,64,130]{2,1,0:T(8,128)}) fusion(pred[6,130]{1,0:T(8,128)(4,1)S(1)} %broadcast_and_fusion, f32[64]{0:T(128)S(1)} %copy-done.5, bf16[6,576,130]{1,2,0:T(8,128)(2,1)} %concatenate.44, bf16[576,64,1]{1,0,2:T(8,128)(2,1)} %bitcast.107), kind=kOutput, calls=%fused_computation.24 | convolution fusion | flops 58056960 | bytes 1272844 | tf_op jit(solution)/shard_map/ykx,ko->yox/dot_general | solution.py:30
  57.8 1.9 %fusion.3 = bf16[4,64,128]{1,2,0:T(8,128)(2,1)} fusion(bf16[4,576,128]{2,1,0:T(8,128)(2,1)S(1)} %slice_dynamic-update-slice_fusion, bf16[576,64,1]{1,0,2:T(8,128)(2,1)} %bitcast.103, bf16[8,64,256]{1,2,0:T(8,128)(2,1)S(1)} %bitcast.100), kind=kOutput, calls=%fused_computation.6 | convolution fusion | flops 37847040 | bytes 794624 | tf_op jit(solution)/shard_map/ykx,ko->yox/dot_general | solution.py:30
  59.8 1.6 %copy.46 = bf16[4,64,128]{2,1,0:T(8,128)(2,1)} copy(bf16[4,64,128]{1,2,0:T(8,128)(2,1)} %fusion.3) | data formatting | bytes 131072
  61.6 0.1 fusion.35
  61.9 0.1 fusion.33
  62.1 0.1 fusion.42
  62.3 0.8 copy-done.4
  63.1 0.9 reverse_bitcast_fusion.1
  64.0 0.1 copy.37
  64.1 1.5 %convert_reduce_fusion = (f32[64]{0:T(128)S(1)}, bf16[4,64,128]{2,1,0:T(8,128)(2,1)S(1)}) fusion(f32[6,64,130]{2,1,0:T(8,128)} %get-tuple-element.48, bf16[4,576,128]{2,1,0:T(8,128)(2,1)} %copy-done.4, bf16[576,64,1]{1,0,2:T(8,128)(2,1)S(1)} %bitcast.108), kind=kOutput, calls=%fused_computation.53 | convolution fusion | flops 38469568 | bytes 860416 | tf_op jit(solution)/shard_map/ykx,ko->yox/dot_general | solution.py:30
  65.7 0.7 copy.40
  66.5 1.1 %fusion.4 = f32[576,64]{0,1:T(8,128)S(1)} fusion(bf16[4,576,128]{2,1,0:T(8,128)(2,1)S(1)} %slice_dynamic-update-slice_fusion, bf16[4,64,128]{2,1,0:T(8,128)(2,1)} %field_ref.1), kind=kOutput, calls=%fused_computation.9 | convolution fusion | flops 37785600 | bytes 802816 | tf_op jit(solution)/shard_map/ykx,yox->ko/dot_general | solution.py:44
  67.6 0.9 %fusion.44 = (bf16[4,64,128]{1,2,0:T(8,128)(2,1)S(1)}, bf16[4,64,128]{1,2,0:T(8,128)(2,1)S(1)}, bf16[4,64,128]{1,2,0:T(8,128)(2,1)S(1)}, bf16[4,64,128]{1,2,0:T(...) fusion(bf16[8,64,256]{1,2,0:T(8,128)(2,1)S(1)} %bitcast.101), kind=kLoop, calls=%fused_computation.105 | loop fusion | bytes 1179648 | tf_op jit(solution)/shard_map/slice | solution.py:21
  68.6 1.4 %concatenate.46 = bf16[4,576,128]{1,2,0:T(8,128)(2,1)S(1)} concatenate(bf16[4,64,128]{1,2,0:T(8,128)(2,1)} %get-tuple-element.30, bf16[4,64,128]{1,2,0:T(8,128)(2,1)} %get-tuple-element.29, bf16[4,64,128]{1,2,0:T(8,128)(2,1)} %get-tuple-element.28, bf16[4,64,128]{1,2,0:T(8,128)(2,1)} %get-tuple-element.27, bf16[4,64,128]{1,2,0:T(8,128)(2,1)} %get-tuple-element.31, ...), dimensions={1} | concatenate | bytes 1179648 | tf_op jit(solution)/shard_map/concatenate | solution.py:25
  70.0 0.2 fusion.5
  70.4 0.1 copy.57
  70.5 18.8 %shard_map.165 = (f32[32,24,128]{2,1,0:T(8,128)S(1)}, bf16[3,6,64,128]{3,2,1,0:T(8,128)(2,1)S(1)}) custom-call(f32[32,24,128]{2,1,0:T(8,128)S(1)} %bitcast.96, bf16[4,64,128]{2,1,0:T(8,128)(2,1)S(1)} %get-tuple-element.50.field_ref), custom_call_target="tpu_custom_call" | custom-call | tf_op jit(solution)/shard_map/pallas_call | solution.py:216
  90.3 0.9 reverse_bitcast_fusion
  91.2 0.1 copy.44
  91.3 0.9 fusion.7
  92.2 0.9 fusion.46
  93.1 0.5 slice_bitcast_fusion.6
  (45 shorter events, 2.2 us)
Async XLA Ops:
  0.6 1.7 %copy-start = (bf16[8,64,2048]{2,1,0:T(8,128)(2,1)S(1)}, bf16[8,64,2048]{2,1,0:T(8,128)(2,1)}, u32[]{:S(2)}) copy-start(bf16[8,64,2048]{2,1,0:T(8,128)(2,1)} %param.14) | copy-start | bytes 6291460
  48.3 6.1 %copy-start.5 = (f32[64]{0:T(128)S(1)}, f32[64]{0:T(128)}, u32[]{:S(2)}) copy-start(f32[64]{0:T(128)} %param.23) | copy-start | bytes 772
  54.4 6.9 %copy-start.1 = (bf16[3,6,64,128]{3,2,1,0:T(8,128)(2,1)S(1)}, bf16[3,6,64,128]{3,2,1,0:T(8,128)(2,1)}, u32[]{:S(2)}) copy-start(bf16[3,6,64,128]{3,2,1,0:T(8,128)(2,1)} %get-tuple-element.10) | copy-start | bytes 884740
  62.2 0.8 copy-start.4
  67.6 2.7 %copy-start.3 = (f32[1,128]{0,1:T(8,128)S(1)}, f32[1,128]{0,1:T(8,128)}, u32[]{:S(2)}) copy-start(f32[1,128]{0,1:T(8,128)} %copy.40) | copy-start | bytes 1540
  68.6 22.8 %copy-start.2 = (bf16[4,64,128]{2,1,0:T(8,128)(2,1)S(1)}, bf16[4,64,128]{2,1,0:T(8,128)(2,1)}, u32[]{:S(2)}) copy-start(bf16[4,64,128]{2,1,0:T(8,128)(2,1)} %field_ref.1) | copy-start | bytes 196612

commit v5 on v4

--- a/solution.py
+++ b/solution.py
@@ -33,6 +33,21 @@
         weight.reshape(-1, weight.shape[2]),
         preferred_element_type=jnp.float32,
     )
+
+
+def conv_by_rows(padded, weight, height, width):
+    columns = jnp.concatenate([padded[:, :, tap : tap + width] for tap in range(3)], axis=1)
+    rows = weight.reshape(3, -1, weight.shape[2])
+    total = None
+    for tap in range(3):
+        term = jnp.einsum(
+            "ykx,ko->yox",
+            columns[tap : tap + height],
+            rows[tap],
+            preferred_element_type=jnp.float32,
+        )
+        total = term if total is None else total + term
+    return total
 
 
 def flipped(weight):
@@ -565,7 +580,7 @@
     widened = fine_wide[:, :, 16 * R - 2 : 16 * R + width + 2]
     upsampled = fine_wide[2 : 2 + height, :, 16 * R : 16 * R + width]
     bias_cols = bias1[None, :, None]
-    pre_wide = conv_padded(widened, conv1, height + 2, width + 2) + bias_cols
+    pre_wide = conv_by_rows(widened, conv1, height + 2, width + 2) + bias_cols
     row_ids = lax.axis_index("band") * height + jnp.arange(height + 2) - 1
     col_ids = lax.axis_index("var") * width + jnp.arange(width + 2) - 1
     rows_inside = (row_ids >= 0) & (row_ids < height * band_count)
@@ -578,7 +593,7 @@
         conv_padded(active_pad, conv2, height, width) + upsampled.astype(jnp.float32)
     ).astype(jnp.bfloat16)
     cotangent_pad = padded_from(rim)
-    d_active = conv_padded(cotangent_pad, flipped(conv2), height, width)
+    d_active = conv_by_rows(cotangent_pad, flipped(conv2), height, width)
     d_pre = jax.vjp(jax.nn.gelu, pre)[1](d_active)[0].astype(jnp.bfloat16)
     factor = 1.0 / math.sqrt(height * band_count * width * var_count)
     first_terms = weight_grad(fine_pad, d_pre).reshape(9 * C, C) * factor
@@ -590,7 +605,7 @@
         jnp.concatenate([terms, bias_row], axis=0), d_pre, band_count, var_count
     )
     grad_fine = (
-        cotangent.astype(jnp.float32) + conv_padded(d_pre_pad, flipped(conv1), height, width)
+        cotangent.astype(jnp.float32) + conv_by_rows(d_pre_pad, flipped(conv1), height, width)
     ).astype(jnp.bfloat16)
     grad_conv1 = summed[: 9 * C, :C].reshape(9, C, C)
     grad_conv2 = summed[: 9 * C, C:].reshape(9, C, C)

time: 94.3 us -> 93.9 us (level)
  the two profiles are of different devices: /device:TPU:0 before, /device:TPU:25 now
where the time goes in v5:
time: 93.9 us; the launch traced here: 92.1 us
  Pallas kernels  61.5 us (65%)
  local copies, waits for them, and re-layouts  17.3 us (18%)
  matrix products  11.4 us (12%)
  other arithmetic  1.05 us (1%)
    pallas_call x1, Pallas kernels, token_stage(): pl.pallas_call(functools.partial(token_kernel, bands, heads, parts), out_...  42.2 us
    pallas_call x1, Pallas kernels, sum_everywhere(): pl.pallas_call(functools.partial(sum_kernel, count, var_count), out_shape...  19.2 us
    dot_general x9, matrix products, conv_by_rows(): jnp.einsum('ykx,ko->yox', columns[tap:tap + height], rows[tap], preferred...  8.63 us
    slice x9, local copies, waits for them, and re-layouts, conv_by_rows(): rows[tap]  4.68 us
    unnamed x30, local copies, waits for them, and re-layouts  2.83 us

profile of v5, /device:TPU:25, one launch (start us, length us, event | category | flops | bytes accessed | tf_op | source)
XLA Modules:
  0.0 92.1 jit_solution(13496146915814889119)
XLA Ops:
  0.8 1.0 %fusion.45 = (bf16[3,64,64]{2,1,0:T(8,128)(2,1)S(1)}, bf16[3,64,64]{2,1,0:T(8,128)(2,1)S(1)}, bf16[3,64,64]{2,1,0:T(8,128)(2,1)S(1)}) fusion(bf16[9,64,64]{2,1,0:T(8,128)(2,1)} %param.22), kind=kLoop, calls=%fused_computation.82 | loop fusion | bytes 147456 | tf_op jit(solution)/shard_map/slice | solution.py:46
  1.7 1.0 %copy.38 = bf16[1,64,8,64]{3,2,1,0:T(8,128)(2,1)S(1)} copy(bf16[1,64,8,64]{3,1,0,2:T(8,128)(2,1)} %bitcast.117) | data formatting | bytes 131072 | tf_op jit(solution)/shard_map/transpose | solution.py:562
  2.9 0.9 reduce_sum.18
  3.8 1.2 %fusion.mix_ref = bf16[64,2048]{1,0:T(8,128)(2,1)} fusion(bf16[64,512]{1,0:T(8,128)(2,1)S(1)} %reshape.106, bf16[512,2048]{1,0:T(8,128)(2,1)S(1)} %bitcast.104, f32[2048]{0:T(1024)S(1)} %reduce_sum.18), kind=kOutput, calls=%fused_computation.1 | convolution fusion | flops 134479872 | bytes 2433024 | tf_op jit(solution)/shard_map/dot_general | solution.py:565
  4.9 42.2 %shard_map.164 = (bf16[64,2048]{1,0:T(8,128)(2,1)}, bf16[3,6,64,128]{3,2,1,0:T(8,128)(2,1)}) custom-call(bf16[64,2048]{1,0:T(8,128)(2,1)} %fusion.mix_ref, f32[1,2048]{1,0:T(1,128)} %bitcast.125, bf16[4,64,128]{2,1,0:T(8,128)(2,1)} %field_ref.1, bf16[2048,1024]{1,0:T(8,128)(2,1)} %wq_any.1, bf16[2048,1024]{1,0:T(8,128)(2,1)} %wk_any.1, ...), custom_call_target="tpu_custom_call" | custom-call | tf_op jit(solution)/shard_map/pallas_call | solution.py:530
  47.2 1.5 %reshape.108 = bf16[64,8,4,64]{3,2,1,0:T(4,128)(2,1)S(1)} reshape(bf16[64,2048]{1,0:T(8,128)(2,1)} %get-tuple-element.9) | data formatting | bytes 524288 | tf_op jit(solution)/shard_map/reshape | solution.py:578
  49.0 0.4 fusion.39
  49.4 0.4 convolution_add_fusion.2
  49.8 0.2 copy-done.9
  50.1 1.2 %fusion.19 = (bf16[6,64,130]{2,1,0:T(8,128)(2,1)S(1)}, f32[6,64,130]{2,1,0:T(8,128)}) fusion(pred[6,130]{1,0:T(8,128)(4,1)S(1)} %broadcast_and_fusion, f32[64]{0:T(128)S(1)} %copy-done.9, f32[6,130,64]{1,2,0:T(8,128)S(1)} %convolution_add_fusion.2, bf16[192,64,1]{1,0,2:T(8,128)(2,1)S(1)} %bitcast.118, bf16[8,64,130]{1,2,0:T(8,128)(2,1)S(1)} %get-tuple-element.33, ...), kind=kOutput, calls=%fused_computation.31 | convolution fusion | flops 20966400 | bytes 924172 | tf_op jit(solution)/shard_map/ykx,ko->yox/dot_general | solution.py:43
  52.2 1.0 %fusion.4 = bf16[4,64,128]{1,2,0:T(8,128)(2,1)} fusion(bf16[4,576,128]{2,1,0:T(8,128)(2,1)S(1)} %slice_dynamic-update-slice_fusion, bf16[576,64,1]{1,0,2:T(8,128)(2,1)S(1)} %bitcast.112, bf16[8,64,256]{1,2,0:T(8,128)(2,1)S(1)} %bitcast.109), kind=kOutput, calls=%fused_computation.8 | convolution fusion | flops 37847040 | bytes 794624 | tf_op jit(solution)/shard_map/ykx,ko->yox/dot_general | solution.py:30
  53.2 1.6 %copy.64 = bf16[4,64,128]{2,1,0:T(8,128)(2,1)} copy(bf16[4,64,128]{1,2,0:T(8,128)(2,1)} %fusion.4) | data formatting | bytes 131072
  54.9 0.6 fusion.43
  55.5 0.7 copy.58
  56.2 0.7 copy.47
  57.0 1.0 %slice_bitcast_fusion.5 = (bf16[6,64,1]{2,1,0:T(8,128)(2,1)S(1)}, bf16[6,64,1]{2,1,0:T(8,128)(2,1)S(1)}) fusion(bf16[3,6,64,128]{3,2,1,0:T(8,128)(2,1)} %get-tuple-element.10), kind=kLoop, calls=%fused_computation.58 | loop fusion | bytes 3072 | tf_op jit(solution)/shard_map/squeeze | solution.py:118
  58.0 1.0 %slice_bitcast_fusion.4 = bf16[6,64,128]{2,1,0:T(8,128)(2,1)S(1)} fusion(bf16[3,6,64,128]{3,2,1,0:T(8,128)(2,1)} %get-tuple-element.10), kind=kLoop, calls=%fused_computation.57 | loop fusion | bytes 196608 | tf_op jit(solution)/shard_map/squeeze | solution.py:118
  59.0 1.7 %fusion.33 = f32[4,128,64]{1,2,0:T(8,128)} fusion(bf16[192,64,1]{1,0,2:T(8,128)(2,1)} %bitcast.120, bf16[6,64,1]{2,1,0:T(8,128)(2,1)S(1)} %get-tuple-element.40, bf16[6,64,128]{2,1,0:T(8,128)(2,1)S(1)} %slice_bitcast_fusion.4, bf16[6,64,1]{2,1,0:T(8,128)(2,1)S(1)} %get-tuple-element.39), kind=kOutput, calls=%fused_computation.74 | convolution fusion | flops 14057472 | bytes 255488 | tf_op jit(solution)/shard_map/ykx,ko->yox/dot_general | solution.py:43
  60.7 0.7 copy.49
  61.5 1.9 %convolution_add_fusion.6 = f32[4,128,64]{1,2,0:T(8,128)} fusion(f32[4,128,64]{1,2,0:T(8,128)} %fusion.33, bf16[192,64,1]{1,0,2:T(8,128)(2,1)} %bitcast.123, bf16[6,64,1]{2,1,0:T(8,128)(2,1)} %copy-done.7, bf16[6,64,128]{2,1,0:T(8,128)(2,1)S(1)} %slice_bitcast_fusion.4, bf16[6,64,1]{2,1,0:T(8,128)(2,1)S(1)} %get-tuple-element.39), kind=kOutput, calls=%fused_computation.19 | convolution fusion | flops 14090240 | bytes 386560 | tf_op jit(solution)/shard_map/ykx,ko->yox/dot_general | solution.py:43
  63.4 0.7 copy.51
  64.1 1.5 %convert_reduce_fusion = (f32[64]{0:T(128)S(1)}, bf16[4,64,128]{2,1,0:T(8,128)(2,1)S(1)}) fusion(f32[6,64,130]{2,1,0:T(8,128)} %get-tuple-element.51, f32[4,128,64]{1,2,0:T(8,128)} %convolution_add_fusion.6, bf16[192,64,1]{1,0,2:T(8,128)(2,1)} %bitcast.121, bf16[6,64,1]{2,1,0:T(8,128)(2,1)} %copy-done.7, bf16[6,64,128]{2,1,0:T(8,128)(2,1)S(1)} %slice_bitcast_fusion.4, ...), kind=kOutput, calls=%fused_computation.52 | convolution fusion | flops 14811072 | bytes 452352 | tf_op jit(solution)/shard_map/ykx,ko->yox/dot_general | solution.py:43
  65.6 0.7 copy.54
  66.4 0.3 fusion.5
  66.7 1.0 %fusion.40 = (bf16[4,64,128]{1,2,0:T(8,128)(2,1)S(1)}, bf16[4,64,128]{1,2,0:T(8,128)(2,1)S(1)}, bf16[4,64,128]{1,2,0:T(8,128)(2,1)S(1)}, bf16[4,64,128]{1,2,0:T(...) fusion(bf16[8,64,256]{1,2,0:T(8,128)(2,1)S(1)} %bitcast.110), kind=kLoop, calls=%fused_computation.77 | loop fusion | bytes 1179648 | tf_op jit(solution)/shard_map/slice | solution.py:21
  67.6 1.4 %concatenate.38 = bf16[4,576,128]{1,2,0:T(8,128)(2,1)S(1)} concatenate(bf16[4,64,128]{1,2,0:T(8,128)(2,1)} %get-tuple-element.30, bf16[4,64,128]{1,2,0:T(8,128)(2,1)} %get-tuple-element.29, bf16[4,64,128]{1,2,0:T(8,128)(2,1)} %get-tuple-element.28, bf16[4,64,128]{1,2,0:T(8,128)(2,1)} %get-tuple-element.27, bf16[4,64,128]{1,2,0:T(8,128)(2,1)} %get-tuple-element.31, ...), dimensions={1} | concatenate | bytes 1179648 | tf_op jit(solution)/shard_map/concatenate | solution.py:25
  69.6 19.2 %shard_map.165 = (f32[32,24,128]{2,1,0:T(8,128)S(1)}, bf16[3,6,64,128]{3,2,1,0:T(8,128)(2,1)S(1)}) custom-call(f32[32,24,128]{2,1,0:T(8,128)S(1)} %bitcast.105, bf16[4,64,128]{2,1,0:T(8,128)(2,1)S(1)} %get-tuple-element.53.field_ref), custom_call_target="tpu_custom_call" | custom-call | tf_op jit(solution)/shard_map/pallas_call | solution.py:231
  89.0 0.3 fusion.37
  89.4 0.3 convolution_add_fusion.4
  89.8 0.9 fusion.10
  90.7 0.9 fusion.42
  91.6 0.5 slice_bitcast_fusion.6
  (47 shorter events, 2.3 us)
Async XLA Ops:
  0.6 2.3 %copy-start = (bf16[8,64,2048]{2,1,0:T(8,128)(2,1)S(1)}, bf16[8,64,2048]{2,1,0:T(8,128)(2,1)}, u32[]{:S(2)}) copy-start(bf16[8,64,2048]{2,1,0:T(8,128)(2,1)} %param.14) | copy-start | bytes 6291460
  49.4 0.7 copy-start.9
  51.3 0.9 copy-start.2
  51.3 3.5 %copy-start.1 = (bf16[9,64,64]{2,1,0:T(8,128)(2,1)S(1)}, bf16[9,64,64]{2,1,0:T(8,128)(2,1)}, u32[]{:S(2)}) copy-start(bf16[9,64,64]{2,1,0:T(8,128)(2,1)} %param.22) | copy-start | bytes 221188
  58.0 1.0 %copy-start.7 = (bf16[6,64,1]{2,1,0:T(8,128)(2,1)}, bf16[6,64,1]{2,1,0:T(8,128)(2,1)S(1)}, u32[]{:S(2)}) copy-start(bf16[6,64,1]{2,1,0:T(8,128)(2,1)S(1)} %get-tuple-element.40) | copy-start | bytes 2308
  58.0 3.4 %copy-start.6 = (bf16[6,64,1]{2,1,0:T(8,128)(2,1)}, bf16[6,64,1]{2,1,0:T(8,128)(2,1)S(1)}, u32[]{:S(2)}) copy-start(bf16[6,64,1]{2,1,0:T(8,128)(2,1)S(1)} %get-tuple-element.39) | copy-start | bytes 2308
  63.4 3.0 %copy-start.3 = (bf16[4,64,128]{2,1,0:T(8,128)(2,1)S(1)}, bf16[4,64,128]{2,1,0:T(8,128)(2,1)}, u32[]{:S(2)}) copy-start(bf16[4,64,128]{2,1,0:T(8,128)(2,1)} %field_ref.1) | copy-start | bytes 196612
  67.6 1.7 %copy-start.4 = (f32[1,128]{0,1:T(8,128)S(1)}, f32[1,128]{0,1:T(8,128)}, u32[]{:S(2)}) copy-start(f32[1,128]{0,1:T(8,128)} %copy.54) | copy-start | bytes 1540
  69.6 19.4 %copy-start.8 = (bf16[3,64,64]{2,1,0:T(8,128)(2,1)S(1)}, bf16[3,64,64]{2,1,0:T(8,128)(2,1)}, u32[]{:S(2)}) copy-start(bf16[3,64,64]{2,1,0:T(8,128)(2,1)} %copy.58) | copy-start | bytes 73732
  69.6 19.7 %copy-start.5 = (bf16[3,64,64]{1,2,0:T(8,128)(2,1)S(1)}, bf16[3,64,64]{1,2,0:T(8,128)(2,1)}, u32[]{:S(2)}) copy-start(bf16[3,64,64]{1,2,0:T(8,128)(2,1)} %get-tuple-element.42) | copy-start | bytes 73732
